TPU v7x, 128 devices: a whole 4x4x4 slice. The times are simulated.
128 devices in a mesh: sec: 16 (over z, y), dp: 8 (over x, core).
Axes of the slice: x: 4, y: 4, z: 4, core: 2. Of those that a mesh axis runs over, the one named last changes fastest.
Arguments:
- range_features: bfloat16 [8, 1024, 64, 256], P('dp', 'sec'), may hold values from -6 to 6
- conv_weight: bfloat16 [3, 256, 256], replicated, may hold values from -0.21875 to 0.21875
- cell_cycle: int32 [1024, 64, 1], P('sec'), may hold values from 0 to 15; in each aligned block of 4096 rows (0 to 4095, 4096 to 8191, ..., all dimensions but the last counted through in order) at most 768 rows name the same one
- cell_token: int32 [1024, 64], P('sec'), may hold values from 0 to 255
- in_weight: bfloat16 [256, 1024], replicated, may hold values from -0.375 to 0.375
- qkv_weight: bfloat16 [1024, 3072], replicated, may hold values from -0.1875 to 0.1875
- out_weight: bfloat16 [1024, 1024], replicated, may hold values from -0.1875 to 0.1875
- voxel_weight: bfloat16 [1024, 2048], replicated, may hold values from -0.1875 to 0.1875
- density_weight: bfloat16 [1024, 16], replicated, may hold values from -0.1875 to 0.1875
- ray_embed: bfloat16 [16384, 128], replicated, may hold values from -1.5 to 1.5
- block_ids: int32 [16, 128, 4], P('sec'), may hold values from 0 to 31
- density_cotangent: bfloat16 [8, 4096, 16], P('dp', 'sec'), may hold values from -6 to 6
Outputs:
- depth: float32 [8, 16384], P('dp', 'sec')
- density_grad: float32 [16, 1024], replicated
Inputs may be any that keep to these rules, and one draw needn't show every extreme that they name: `cell_cycle`: among the cells of one sector (4096 cells in a row), no cycle is named more than 768 times, a bound that some block reaches.
All inputs are finite; a program needn't handle non-finite values.
Results may differ from a plain program's by a relative error of at most 0.0056.
The roundings to bfloat16 on the way count: a program that leaves them out, or rounds other values in their place, can miss the bound.
Values may be sent and summed in bfloat16 or wider, within the bound.
A program may use at most 256 MiB of HBM per device.

v0:
```python
import jax
import jax.numpy as jnp
from jax import lax
from jax.sharding import PartitionSpec as P

D = 1024
HEADS = 16
HEAD = 64
EMB = 128
KB = 4
TOKB_DEV = 256


def extended(cells, sides, width):
    for axis, dim in sides:
        count = lax.axis_size(axis)
        head = lax.slice_in_dim(cells, 0, width, axis=dim)
        tail = lax.slice_in_dim(cells, cells.shape[dim] - width, cells.shape[dim], axis=dim)
        cells = jnp.concatenate(
            [
                lax.ppermute(tail, axis, [(i, (i + 1) % count) for i in range(count)]),
                cells,
                lax.ppermute(head, axis, [((i + 1) % count, i) for i in range(count)]),
            ],
            axis=dim,
        )
    return cells


def carried_in(value, axis, join, neutral):
    count, mine = (lax.axis_size(axis), lax.axis_index(axis))
    pieces = jax.tree.map(lambda part: lax.all_gather(part, axis), value)
    subtotal = jax.tree.map(
        lambda part, zero: jnp.full_like(part, 0) + jnp.asarray(zero, part.dtype), value, neutral
    )

    def step(position, subtotal):
        longer = join(subtotal, jax.tree.map(lambda part: part[position], pieces))
        return jax.tree.map(lambda new, old: jnp.where(position < mine, new, old), longer, subtotal)

    return lax.fori_loop(0, count - 1, step, subtotal)


def add_values(left, right):
    return left + right


def shards(
    range_features,
    conv_weight,
    cell_cycle,
    cell_token,
    in_weight,
    qkv_weight,
    out_weight,
    voxel_weight,
    density_weight,
    ray_embed,
    block_ids,
    density_cotangent,
):
    feats = range_features[0]
    az_dev, beams, width = feats.shape
    n_sec = lax.axis_size("sec")
    cells = az_dev * beams
    padded = extended(feats, (("sec", 0),), 1)
    total = jnp.zeros((cells, width), jnp.float32)
    for k in range(3):
        total = total + jnp.dot(
            padded[k : k + az_dev].reshape(cells, width),
            conv_weight[k],
            preferred_element_type=jnp.float32,
        )
    encoded = (feats.reshape(cells, width).astype(jnp.float32) + jax.nn.gelu(total)).astype(
        jnp.bfloat16
    )
    cycle = cell_cycle.reshape(-1)
    token = cell_token.reshape(-1)
    tokb = TOKB_DEV
    cap = 3 * cells // n_sec
    member = (cycle[:, None] == jnp.arange(n_sec, dtype=jnp.int32)[None, :]).astype(jnp.int32)
    running = jnp.cumsum(member, axis=0)
    place = jnp.take_along_axis(running, cycle[:, None], axis=1)[:, 0] - 1
    target = cycle * cap + place
    outbox = jnp.zeros((n_sec * cap, width), jnp.bfloat16).at[target].set(encoded)
    out_ids = jnp.full((n_sec * cap,), -1, jnp.int32).at[target].set(token)
    inbox = lax.all_to_all(
        outbox.reshape(n_sec, cap, width), "sec", split_axis=0, concat_axis=0, tiled=True
    )
    in_ids = lax.all_to_all(
        out_ids.reshape(n_sec, cap), "sec", split_axis=0, concat_axis=0, tiled=True
    )
    picks = in_ids.reshape(-1)[None, :] == jnp.arange(tokb, dtype=jnp.int32)[:, None]
    sums = jnp.dot(
        picks.astype(jnp.bfloat16), inbox.reshape(-1, width), preferred_element_type=jnp.float32
    )
    counts = jnp.sum(picks.astype(jnp.float32), axis=1)
    pooled = (sums / jnp.sqrt(counts + 1.0)[:, None]).astype(jnp.bfloat16)
    lifted = jnp.dot(pooled, in_weight, preferred_element_type=jnp.float32)
    normed = (lifted * lax.rsqrt(jnp.mean(lifted * lifted, axis=-1, keepdims=True) + 1e-06)).astype(
        jnp.bfloat16
    )
    scale = HEAD ** (-0.5)
    query = (
        jnp.dot(normed, qkv_weight[:, :D], preferred_element_type=jnp.float32)
        .astype(jnp.bfloat16)
        .reshape(tokb, HEADS, HEAD)
    )
    key_value = jnp.dot(normed, qkv_weight[:, D:], preferred_element_type=jnp.float32).astype(
        jnp.bfloat16
    )
    keys = lax.all_gather(key_value[:, :D], "sec", axis=0, tiled=True)
    values = lax.all_gather(key_value[:, D:], "sec", axis=0, tiled=True)
    rows = keys.shape[0]
    keys = keys.reshape(rows, HEADS, HEAD)
    values = values.reshape(rows, HEADS, HEAD)
    scores = jnp.einsum("qhd,khd->hqk", query, keys, preferred_element_type=jnp.float32) * scale
    expo = jnp.exp(scores)
    mass = jnp.sum(expo, axis=-1)
    acc = jnp.einsum(
        "hqk,khd->hqd", expo.astype(jnp.bfloat16), values, preferred_element_type=jnp.float32
    )
    mass, acc = (mass, acc)
    ctx = (acc / mass[..., None]).transpose(1, 0, 2).reshape(tokb, D).astype(jnp.bfloat16)
    mixed = (
        normed.astype(jnp.float32) + jnp.dot(ctx, out_weight, preferred_element_type=jnp.float32)
    ).astype(jnp.bfloat16)
    voxel = jnp.dot(mixed, voxel_weight, preferred_element_type=jnp.float32).astype(jnp.bfloat16)
    vblocks = voxel.reshape(-1, 128, EMB)
    logit = jnp.dot(mixed, density_weight, preferred_element_type=jnp.float32)
    dblocks = jax.nn.softplus(logit).reshape(-1, 128)
    all_rays = ray_embed.shape[0]
    bundles = all_rays // 128
    ray_blocks = ray_embed.reshape(bundles, 128, EMB)
    cycle_ids = block_ids[0]

    def one_bundle(args):
        rays_here, ids_here = args
        chosen = vblocks[ids_here].reshape(KB * 128, EMB)
        dens = dblocks[ids_here].reshape(KB * 128)
        scores = lax.dot_general(
            rays_here, chosen, (((1,), (1,)), ((), ())), preferred_element_type=jnp.float32
        )
        return jnp.sum(jax.nn.softplus(scores) * dens[None, :], axis=-1)

    tau = lax.map(one_bundle, (ray_blocks, cycle_ids), batch_size=16).reshape(all_rays) * (
        4.0 / (n_sec * KB * 128)
    )
    here = lax.axis_index("sec")
    before = carried_in(tau, "sec", add_values, jnp.zeros_like(tau))
    dist = here.astype(jnp.float32) + 0.5
    contrib = dist * jnp.exp(-before) * (1.0 - jnp.exp(-tau))
    depth = lax.psum_scatter(contrib, "sec", scatter_dimension=0, tiled=True)
    term = density_cotangent[0].astype(jnp.float32) * jax.nn.sigmoid(logit)
    part = jnp.dot(term.T, mixed.astype(jnp.float32), precision=lax.Precision.HIGHEST)
    grad = lax.psum(part, ("sec", "dp"))
    return (depth[None, :], grad)


def solution(mesh):
    placed = (
        P("dp", "sec", None, None),
        P(),
        P("sec", None, None),
        P("sec", None),
        P(),
        P(),
        P(),
        P(),
        P(),
        P(),
        P("sec", None, None),
        P("dp", "sec", None),
    )
    return jax.shard_map(
        shards, mesh=mesh, in_specs=placed, out_specs=(P("dp", "sec"), P()), check_vma=False
    )
```

profile of v0, /device:TPU:1, one launch (start us, length us, event | category | flops | bytes accessed | tf_op | source)
XLA Modules:
  0.0 799.0 jit_solution(7769032169629261400)
XLA Ops:
  8.1 2.1 collective-permute-start
  10.2 5.0 collective-permute-start.1
  16.9 4.6 reduce-window.6
  23.2 1.5 reduce.11
  25.6 33.0 %gather_fusion.2 = s32[4096]{0:T(1024)S(1)} fusion(s32[4096,16]{0,1:T(8,128)S(1)} %bitcast.107, s32[4096]{0:T(1024)S(1)} %bitcast.108), kind=kCustom, calls=%fused_computation.2 | custom fusion | bytes 65536 | tf_op jit(solution)/shard_map/jit(take_along_axis)/gather | solution.py:83
  58.7 16.1 %scatter_custom_fusion = s32[12288]{0:T(1024)} fusion(s32[4096]{0:T(1024)S(1)} %bitcast.134, s32[4096]{0:T(1024)S(1)} %reshape.325, s32[]{:T(128)} %constant.90.clone.1), kind=kCustom, calls=%fused_computation.87 | custom fusion | bytes 49156 | tf_op jit(solution)/shard_map/scatter | solution.py:86
  74.8 3.5 all-to-all-start
  78.3 2.4 fusion.50
  81.8 3.3 fusion.21
  85.1 22.0 %scatter_custom_fusion.1 = bf16[12288,256]{1,0:T(8,128)(2,1)} fusion(s32[4096]{0:T(1024)S(1)} %bitcast.135, bf16[4096,256]{1,0:T(8,128)(2,1)} %fusion.21, bf16[]{:T(256)} %constant.96.clone.1), kind=kCustom, calls=%fused_computation.42 | custom fusion | bytes 6291968 | tf_op jit(solution)/shard_map/scatter | solution.py:85
  107.1 6.8 all-to-all-start.1
  114.1 2.1 convert_reduce_fusion
  116.2 89.2 %all-to-all-done.1 = bf16[16,768,256]{2,1,0:T(8,128)(2,1)} async-done(((bf16[16,768,256]{2,1,0:T(8,128)(2,1)}), bf16[16,768,256]{2,1,0:T(8,128)(2,1)}, u32[]{:S(2)}, u32[]{:S(2)}) %all-to-all-start.1) | async-done | bytes 6291488 | tf_op jit(solution)/shard_map/all_to_all | solution.py:87
  205.4 6.0 multiply_reduce_fusion.1
  211.5 1.3 multiply_convert_fusion
  212.9 3.4 fusion.26
  218.3 3.1 fusion.34
  221.4 1.2 copy.31
  222.6 66.8 %all-gather.5.cloned.1.call-done = bf16[4096,1024]{1,0:T(8,128)(2,1)} async-done(((bf16[256,1024]{1,0:T(8,128)(2,1)}), bf16[4096,1024]{1,0:T(8,128)(2,1)}) %all-gather.5.cloned.1.call-update) | async-done | bytes 8388624 | tf_op jit(solution)/shard_map/all_gather | solution.py:112
  289.5 12.0 %copy.32 = bf16[4096,1024]{0,1:T(8,128)(2,1)} copy(bf16[4096,1024]{1,0:T(8,128)(2,1)} %all-gather.5.cloned.1.call-done) | data formatting | bytes 16777216 | tf_op jit(solution)/shard_map/all_gather | solution.py:112
  301.5 28.2 %fusion.5 = (f32[16,256]{1,0:T(8,128)S(1)}, f32[16,256,4096]{2,1,0:T(8,128)}) fusion(bf16[256,16,64]{0,2,1:T(8,128)(2,1)S(1)} %bitcast.119, bf16[4096,16,64]{0,2,1:T(8,128)(2,1)} %bitcast.110), kind=kOutput, calls=%fused_computation.20 | convolution fusion | flops 2181033984 | bytes 76038144 | tf_op jit(solution)/shard_map/qhd,khd->hqk/dot_general | solution.py:117
  329.6 32.5 %all-gather.7.cloned.1.call-done = bf16[4096,1024]{1,0:T(8,128)(2,1)} async-done(((bf16[256,1024]{1,0:T(8,128)(2,1)}), bf16[4096,1024]{1,0:T(8,128)(2,1)}) %all-gather.7.cloned.1.call-update) | async-done | bytes 8388624 | tf_op jit(solution)/shard_map/all_gather | solution.py:113
  362.2 12.0 %copy.33 = bf16[4096,1024]{0,1:T(8,128)(2,1)} copy(bf16[4096,1024]{1,0:T(8,128)(2,1)} %all-gather.7.cloned.1.call-done) | data formatting | bytes 16777216 | tf_op jit(solution)/shard_map/all_gather | solution.py:113
  374.2 25.6 %fusion.44 = bf16[256,16,64]{0,2,1:T(8,128)(2,1)S(1)} fusion(bf16[4096,16,64]{0,2,1:T(8,128)(2,1)} %bitcast.111, f32[16,256,4096]{2,1,0:T(8,128)} %get-tuple-element.181, f32[256,16]{0,1:T(8,128)S(1)} %bitcast.126), kind=kOutput, calls=%fused_computation.58 | convolution fusion | flops 2181562368 | bytes 76038144 | tf_op jit(solution)/shard_map/hqk,khd->hqd/dot_general | solution.py:120
  402.1 2.3 convolution_convert_fusion
  404.4 1.6 reshape.294
  406.1 98.2 %while.24 = (s32[]{:T(128)}, f32[8,16,128]{2,1,0:T(8,128)S(1)}, bf16[8,16,128,128]{3,2,1,0:T(8,128)(2,1)}, s32[8,16,4]{1,0,2:T(8,128)S(1)}, bf16[32,128,128]{2,1...) while((s32[]{:T(128)}, f32[8,16,128]{2,1,0:T(8,128)S(1)}, bf16[8,16,128,128]{3,2,1,0:T(8,128)(2,1)}, ...), condition=%wide.region_9.10_spmd, body=%wide.region_7.9_spmd.sunk | while | flops 285146304 | bytes 15662421 | solution.py:146
  406.4 2.1 gather_fusion
  408.5 4.4 fusion.93
  413.5 4.9 multiply_reduce_fusion.3
  418.6 2.1 gather_fusion
  420.8 4.4 fusion.93
  425.8 4.9 multiply_reduce_fusion.3
  430.9 2.1 gather_fusion
  433.0 4.4 fusion.93
  438.1 4.9 multiply_reduce_fusion.3
  443.2 2.1 gather_fusion
  445.3 4.4 fusion.93
  450.3 4.9 multiply_reduce_fusion.3
  455.4 2.1 gather_fusion
  457.6 4.4 fusion.93
  462.6 4.9 multiply_reduce_fusion.3
  467.7 2.1 gather_fusion
  469.8 4.4 fusion.93
  474.9 4.9 multiply_reduce_fusion.3
  480.0 2.1 gather_fusion
  482.1 4.4 fusion.93
  487.1 4.9 multiply_reduce_fusion.3
  492.2 2.1 gather_fusion
  494.4 4.4 fusion.93
  499.4 4.9 multiply_reduce_fusion.3
  505.1 41.1 %all-gather.9.cloned.1.call-done = f32[16,1,16384]{2,1,0:T(1,128)} async-done(((f32[1,1,16384]{2,1,0:T(1,128)}), f32[16,1,16384]{2,1,0:T(1,128)}) %all-gather.9.cloned.1.call-update) | async-done | bytes 1048592 | tf_op jit(solution)/shard_map/all_gather | solution.py:32
  546.2 2.9 copy.41
  549.0 17.1 %while.25 = (s32[]{:T(128)}, f32[16384]{0:T(1024)S(1)}, s32[]{:T(128)}, f32[16,16384]{1,0:T(8,128)}, s32[]{:T(128)}, /*index=5*/s32[]{:T(128)}) while((s32[]{:T(128)}, f32[16384]{0:T(1024)S(1)}, s32[]{:T(128)}, f32[16,16384]{1,0:T(8,128)}, s32[]{:T(128)}, /*index=5*/s32[]{:T(128)}) %tuple.79), condition=%wide.region_11.12_spmd.clone, body=%wide.region_10.11_spmd.clone.sunk | while | flops 49156 | bytes 327773 | solution.py:41
  550.1 1.1 constant_dynamic-slice_fusion.5
  551.3 1.1 constant_dynamic-slice_fusion.5
  552.4 1.1 constant_dynamic-slice_fusion.5
  553.6 1.1 constant_dynamic-slice_fusion.5
  554.7 1.1 constant_dynamic-slice_fusion.5
  555.9 1.1 constant_dynamic-slice_fusion.5
  569.1 78.0 %all-reduce.6.cloned.1.call-done = f32[16384]{0:T(1024)} async-done(((f32[16384]{0:T(1024)}), f32[16384]{0:T(1024)}) %all-reduce.6.cloned.1.call-update) | async-done | bytes 65552
  647.1 1.3 dynamic-slice.1
  648.4 142.6 %all-reduce.4.cloned.1.call-done = f32[16,1024]{1,0:T(8,128)} async-done(((f32[16,1024]{1,0:T(8,128)}), f32[16,1024]{1,0:T(8,128)}) %all-reduce.4.cloned.1.call-update) | async-done | bytes 65552 | tf_op jit(solution)/shard_map/psum | solution.py:156
  791.0 1.5 copy.60
  (155 shorter events, 30.4 us)
Async XLA Ops:
  7.2 392.6 %copy-start = (bf16[1024,1024]{1,0:T(8,128)(2,1)S(1)}, bf16[1024,1024]{1,0:T(8,128)(2,1)}, u32[]{:S(2)}) copy-start(bf16[1024,1024]{1,0:T(8,128)(2,1)} %param.22) | copy-start | bytes 6291460
  8.1 72.7 %collective-permute-start = (bf16[1,64,256]{2,1,0:T(8,128)(2,1)S(1)}, bf16[1,64,256]{2,1,0:T(8,128)(2,1)S(1)}, u32[]{:S(2)}, u32[]{:S(2)}) collective-permute-start(bf16[1,64,256]{2,1,0:T(8,128)(2,1)S(1)} %get-tuple-element.172), channel_id=1, source_target_pairs={{0,8},{8,16},{16,24},{24,32},{32,40},{40,48},{48,56},{56,64},{64,7... | collective-permute-start | bytes 98312 | tf_op jit(solution)/shard_map/ppermute | solution.py:21
  10.2 70.5 %collective-permute-start.1 = (bf16[1,64,256]{2,1,0:T(8,128)(2,1)S(1)}, bf16[1,64,256]{2,1,0:T(8,128)(2,1)S(1)}, u32[]{:S(2)}, u32[]{:S(2)}) collective-permute-start(bf16[1,64,256]{2,1,0:T(8,128)(2,1)S(1)} %get-tuple-element.173), channel_id=1, source_target_pairs={{8,0},{16,8},{24,16},{32,24},{40,32},{48,40},{56,48},{64,56},{72,6... | collective-permute-start | bytes 98312 | tf_op jit(solution)/shard_map/ppermute | solution.py:23
  25.6 52.7 %copy-start.4 = (bf16[3,256,256]{2,1,0:T(8,128)(2,1)S(1)}, bf16[3,256,256]{2,1,0:T(8,128)(2,1)}, u32[]{:S(2)}) copy-start(bf16[3,256,256]{2,1,0:T(8,128)(2,1)} %param.17) | copy-start | bytes 1179652
  74.8 32.3 %all-to-all-start = ((s32[16,1,768]{2,1,0:T(1,128)}), s32[16,1,768]{2,1,0:T(1,128)S(1)}, u32[]{:S(2)}, u32[]{:S(2)}) async-start(s32[16,1,768]{2,1,0:T(1,128)} %bitcast.10), calls=%async_computation | async-start | bytes 98304 | tf_op jit(solution)/shard_map/all_to_all | solution.py:90
  78.3 2.5 copy-start.1
  107.1 98.3 %copy-start.9 = (bf16[256,1024]{1,0:T(8,128)(2,1)S(1)}, bf16[256,1024]{1,0:T(8,128)(2,1)}, u32[]{:S(2)}) copy-start(bf16[256,1024]{1,0:T(8,128)(2,1)} %param.20) | copy-start | bytes 1572868
  107.1 98.3 %all-to-all-start.1 = ((bf16[16,768,256]{2,1,0:T(8,128)(2,1)}), bf16[16,768,256]{2,1,0:T(8,128)(2,1)}, u32[]{:S(2)}, u32[]{:S(2)}) async-start(bf16[16,768,256]{2,1,0:T(8,128)(2,1)} %bitcast.112), calls=%async_computation.1 | async-start | bytes 12582912 | tf_op jit(solution)/shard_map/all_to_all | solution.py:87
  113.9 175.6 %all-gather.5.cloned.1.call-start = ((), (), s32[]{:S(2)}) async-start(), calls=%async_computation.2 | async-start | bytes 8912896 | tf_op jit(solution)/shard_map/all_gather | solution.py:112
  212.8 5.3 copy-start.7
  217.4 144.8 %all-gather.7.cloned.1.call-start = ((), (), s32[]{:S(2)}) async-start(), calls=%async_computation.3 | async-start | bytes 8912896 | tf_op jit(solution)/shard_map/all_gather | solution.py:113
  218.1 328.0 %all-gather.9.cloned.1.call-start = ((), (), s32[]{:S(2)}) async-start(), calls=%async_computation.5 | async-start | bytes 1114112 | tf_op jit(solution)/shard_map/all_gather | solution.py:32
  374.2 26.3 %copy-start.5 = (bf16[1024,16]{0,1:T(8,128)(2,1)S(1)}, bf16[1024,16]{0,1:T(8,128)(2,1)}, u32[]{:S(2)}) copy-start(bf16[1024,16]{0,1:T(8,128)(2,1)} %param.24) | copy-start | bytes 98308
  399.7 2.4 copy-start.8
  400.5 0.8 copy-start.2
  504.3 62.6 %copy-start.3 = (bf16[256,1024]{1,0:T(8,128)(2,1)S(1)}, bf16[256,1024]{1,0:T(8,128)(2,1)}, u32[]{:S(2)}) copy-start(bf16[256,1024]{1,0:T(8,128)(2,1)} %copy-done.2) | copy-start | bytes 1572868
  504.3 62.6 %copy-start.6 = (bf16[1,256,16]{1,2,0:T(8,128)(2,1)S(1)}, bf16[1,256,16]{1,2,0:T(8,128)(2,1)}, u32[]{:S(2)}) copy-start(bf16[1,256,16]{1,2,0:T(8,128)(2,1)} %param.27) | copy-start | bytes 24580
  504.3 63.6 %copy-start.10 = (u32[128]{0:T(128)S(1)}, u32[128]{0:T(128)}, u32[]{:S(2)}) copy-start(u32[128]{0:T(128)} %constant.122) | copy-start | bytes 1540
  505.0 142.1 %all-reduce.6.cloned.1.call-start = ((), (), s32[]{:S(2)}) async-start(), calls=%async_computation.6 | async-start | bytes 131072
  566.8 224.2 %all-reduce.4.cloned.1.call-start = ((), (), s32[]{:S(2)}) async-start(), calls=%async_computation.4 | async-start | bytes 131072 | tf_op jit(solution)/shard_map/psum | solution.py:156
Sparse Core Ops, SparseCore 0:
  217.5 71.9 all-gather.4
  291.6 70.5 all-gather.6
  505.1 40.9 all-gather.8
  566.9 80.1 all-reduce.5
  652.4 138.5 all-reduce.3
where the time goes:
time: 802 us; the launch traced here: 799 us
  waiting for transfers between devices  451 us (56%)
  local copies, waits for them, and re-layouts  151 us (19%)
  matrix products  112 us (14%)
  other arithmetic  50.8 us (6%)
  starting transfers between devices  17.7 us (2%)
  between operations  14.8 us (2%)
    psum x1, waiting for transfers between devices, shards(): grad = lax.psum(part, ('sec', 'dp'))  143 us
    all_to_all x1, waiting for transfers between devices, shards(): lax.all_to_all(outbox.reshape(n_sec, cap, width), 'sec', split_axis=0, co...  89.2 us
    unnamed x6, waiting for transfers between devices  78.8 us
    all_gather x1, waiting for transfers between devices, shards(): keys = lax.all_gather(key_value[:, :D], 'sec', axis=0, tiled=True)  66.8 us
    all_gather x1, waiting for transfers between devices, carried_in(): pieces = jax.tree.map(lambda part: lax.all_gather(part, axis), value)  41.1 us
    reduce_sum x8, other arithmetic, one_bundle(): return jnp.sum(jax.nn.softplus(scores) * dens[None, :], axis=-1)  38.8 us
    dot_general x8, matrix products, one_bundle(): lax.dot_general(rays_here, chosen, (((1,), (1,)), ((), ())), preferred_el...  35.4 us
    gather x1, local copies, waits for them, and re-layouts, shards(): place = jnp.take_along_axis(running, cycle[:, None], axis=1)[:, 0] - 1  33 us
  transfers between devices with their start and end apart: 9, of which 6 were waited for; matrix products, arithmetic and copies ran while one was open for 17% of the time, Pallas kernels for 0%

commit v1 on v0

v1 whole, which is shorter than its diff:
```python
import functools
import math

import jax
import jax.numpy as jnp
from jax import lax
from jax.experimental import pallas as pl
from jax.experimental.pallas import tpu as pltpu
from jax.sharding import PartitionSpec as P

D = 1024
HEADS = 16
HEAD = 64
EMB = 128
KB = 4
TOKB = 256
HEIGHTS = 16
MESH = pl.DeviceIdType.MESH
BF16 = jnp.bfloat16
F32 = jnp.float32
VMEM_LIMIT = 60 * 1024 * 1024
LOG2E = math.log2(math.e)
LN2 = math.log(2.0)


def dot(a, b):
    return jnp.dot(a, b, preferred_element_type=F32)


def dot_nt(a, b):
    return lax.dot_general(a, b, (((1,), (1,)), ((), ())), preferred_element_type=F32)


def greet(axis, n):
    me = lax.axis_index(axis)
    barrier = pltpu.get_barrier_semaphore()

    def hello(i, _):
        pl.semaphore_signal(
            barrier, inc=1, device_id={axis: lax.rem(me + i, n)}, device_id_type=MESH
        )
        return 0

    lax.fori_loop(1, n, hello, 0)


def remote(src, dst, send_sem, recv_sem, axis, peer):
    return pltpu.make_async_remote_copy(
        src_ref=src,
        dst_ref=dst,
        send_sem=send_sem,
        recv_sem=recv_sem,
        device_id={axis: peer},
        device_id_type=MESH,
    )


def swap_halves(x):
    return pltpu.roll(x, HEAD, 1)


def low_lanes(rows):
    return lax.broadcasted_iota(jnp.int32, (rows, 128), 1) < HEAD


def gelu(x):
    inner = math.sqrt(2.0 / math.pi) * (x + 0.044715 * (x * x * x))
    return x * (0.5 * (1.0 + jnp.tanh(inner)))


def softplus2(y):
    return jnp.maximum(y, 0.0) + jnp.log2(1.0 + jnp.exp2(-jnp.abs(y)))


def encode_kernel(
    n,
    cells,
    beams,
    feats,
    conv_hbm,
    gid_ref,
    in_hbm,
    qkv_hbm,
    normed_ref,
    inmsg,
    padded,
    enc,
    outbox,
    inbox,
    cnt_out,
    cnt_in,
    outmsg,
    conv_w,
    in_w,
    qkv_w,
    load_sem,
    halo_send,
    halo_recv,
    box_send,
    box_recv,
    cnt_send,
    cnt_recv,
    msg_send,
    msg_recv,
):
    me = lax.axis_index("sec")
    loads = [
        pltpu.make_async_copy(feats, padded.at[pl.ds(beams, cells)], load_sem.at[0]),
        pltpu.make_async_copy(conv_hbm, conv_w, load_sem.at[1]),
        pltpu.make_async_copy(in_hbm, in_w, load_sem.at[2]),
        pltpu.make_async_copy(qkv_hbm, qkv_w, load_sem.at[3]),
    ]
    for load in loads:
        load.start()
    greet("sec", n)
    pl.semaphore_wait(pltpu.get_barrier_semaphore(), n - 1)
    right, left = lax.rem(me + 1, n), lax.rem(me + n - 1, n)
    halos = [
        remote(
            feats.at[pl.ds(cells - beams, beams)],
            padded.at[pl.ds(0, beams)],
            halo_send.at[0],
            halo_recv.at[0],
            "sec",
            right,
        ),
        remote(
            feats.at[pl.ds(0, beams)],
            padded.at[pl.ds(beams + cells, beams)],
            halo_send.at[1],
            halo_recv.at[1],
            "sec",
            left,
        ),
    ]
    for halo in halos:
        halo.start()

    gid = gid_ref[...]
    tok_hot = jnp.where(
        lax.broadcasted_iota(jnp.int32, (TOKB, cells), 0) == (gid & (TOKB - 1)), 1.0, 0.0
    ).astype(BF16)
    cyc_hot = jnp.where(
        lax.broadcasted_iota(jnp.int32, (n, cells), 0) == (gid // TOKB), 1.0, 0.0
    ).astype(BF16)
    hist = dot_nt(cyc_hot, tok_hot)
    for r in range(n):
        cnt_out[r] = jnp.broadcast_to(hist[r : r + 1, :], (8, TOKB))

    def send_counts(i, _):
        peer = lax.rem(me + i, n)
        remote(
            cnt_out.at[peer], cnt_in.at[me], cnt_send.at[peer], cnt_recv.at[me], "sec", peer
        ).start()
        return 0

    lax.fori_loop(1, n, send_counts, 0)
    cnt_in[me] = cnt_out[me]

    rows = 8 * beams
    chunks = cells // rows

    def encode_chunk(c):
        base = pl.multiple_of(c * rows, rows)
        total = jnp.zeros((rows, enc.shape[1]), F32)
        for k in range(3):
            total = total + dot(padded[pl.ds(base + k * beams, rows), :], conv_w[k])
        own = padded[pl.ds(base + beams, rows), :].astype(F32)
        enc[pl.ds(base, rows), :] = (own + gelu(total)).astype(BF16)

    def inner_chunk(c, _):
        encode_chunk(c)
        return 0

    loads[0].wait()
    loads[1].wait()
    lax.fori_loop(1, chunks - 1, inner_chunk, 0)
    for halo in halos:
        halo.wait()

    def edge_chunk(i, _):
        encode_chunk(i * (chunks - 1))
        return 0

    lax.fori_loop(0, 2, edge_chunk, 0)

    def pool(i, _):
        peer = lax.rem(me + i, n)
        hot = jnp.where(
            lax.broadcasted_iota(jnp.int32, (TOKB, cells), 0) == (gid_ref[...] - peer * TOKB),
            1.0,
            0.0,
        ).astype(BF16)
        part = dot(hot, enc[...]).astype(BF16)

        @pl.when(i < n)
        def _():
            outbox[peer] = part
            remote(
                outbox.at[peer], inbox.at[me], box_send.at[peer], box_recv.at[me], "sec", peer
            ).start()

        @pl.when(i == n)
        def _():
            inbox[me] = part

        return 0

    lax.fori_loop(1, n + 1, pool, 0)

    def arrive(i, _):
        peer = lax.rem(me + n - i, n)
        remote(
            cnt_out.at[peer], cnt_in.at[peer], cnt_send.at[peer], cnt_recv.at[peer], "sec", peer
        ).wait()
        remote(
            outbox.at[peer], inbox.at[peer], box_send.at[peer], box_recv.at[peer], "sec", peer
        ).wait()
        return 0

    lax.fori_loop(1, n, arrive, 0)
    loads[2].wait()
    loads[3].wait()
    sums = inbox[0].astype(F32)
    counts = cnt_in[0]
    for r in range(1, n):
        sums = sums + inbox[r].astype(F32)
        counts = counts + cnt_in[r]
    root = jnp.sqrt(jnp.transpose(counts)[:, 0:1] + 1.0)
    pooled = (sums / root).astype(BF16)
    lifted = dot(pooled, in_w[...])
    normed = (
        lifted * lax.rsqrt(jnp.mean(lifted * lifted, axis=-1, keepdims=True) + 1e-06)
    ).astype(BF16)
    normed_ref[...] = normed

    low, low_half = low_lanes(TOKB), low_lanes(TOKB // 2)
    half = TOKB // 2

    def project(i, _):
        group = lax.rem(me // 4 + i, HEADS // 4)
        column = group * (4 * HEAD)
        q4, k4, v4 = (
            dot(
                normed_ref[...],
                qkv_w[:, pl.ds(pl.multiple_of(part * D + column, 4 * HEAD), 4 * HEAD)],
            )
            for part in range(3)
        )
        for pair in range(2):
            lanes = slice(pair * 128, pair * 128 + 128)
            q, k, v = q4[:, lanes], k4[:, lanes], v4[:, lanes]
            qs, ks, vs = swap_halves(q), swap_halves(k), swap_halves(v)
            head = group * 4 + pair * 2
            outmsg[head, 0:TOKB] = jnp.where(low, q, ks).astype(BF16)
            outmsg[head, TOKB : TOKB + half] = jnp.where(low_half, v[:half], vs[half:]).astype(BF16)
            outmsg[head + 1, 0:TOKB] = jnp.where(low, qs, k).astype(BF16)
            outmsg[head + 1, TOKB : TOKB + half] = jnp.where(low_half, vs[:half], v[half:]).astype(
                BF16
            )
            for one in range(2):
                peer = head + one

                @pl.when(peer != me)
                def _():
                    remote(
                        outmsg.at[peer],
                        inmsg.at[me],
                        msg_send.at[peer],
                        msg_recv.at[me],
                        "sec",
                        peer,
                    ).start()

                @pl.when(peer == me)
                def _():
                    inmsg[me] = outmsg[me]

        return 0

    lax.fori_loop(0, HEADS // 4, project, 0)

    def collect(i, _):
        peer = lax.rem(me + n - i, n)
        remote(
            outmsg.at[peer], inmsg.at[peer], msg_send.at[peer], msg_recv.at[peer], "sec", peer
        ).wait()
        return 0

    lax.fori_loop(1, n, collect, 0)


def attention_kernel(n, msg, inctx, keys, values, outctx, ctx_send, ctx_recv):
    me = lax.axis_index("sec")
    greet("sec", n)
    half = TOKB // 2
    lane = lax.broadcasted_iota(jnp.int32, (half, 128), 1)

    def unpack(r, _):
        base = pl.multiple_of(r * TOKB, TOKB)
        qk = msg[r, 0:TOKB].astype(F32)
        keys[pl.ds(base, TOKB), :] = swap_halves(qk).astype(BF16)
        v = msg[r, TOKB : TOKB + half].astype(F32)
        ones = jnp.where(lane == HEAD, 1.0, 0.0)
        values[pl.ds(base, half), :] = jnp.where(lane < HEAD, v, ones).astype(BF16)
        values[pl.ds(base + half, half), :] = jnp.where(lane < HEAD, swap_halves(v), ones).astype(
            BF16
        )
        return 0

    lax.fori_loop(0, n, unpack, 0)
    pl.semaphore_wait(pltpu.get_barrier_semaphore(), n - 1)
    rows = n * TOKB
    width = 1024
    scale = LOG2E * HEAD ** (-0.5)
    low, low_half = low_lanes(TOKB), low_lanes(half)

    def attend(i, _):
        first = 2 * lax.rem(me // 2 + 1 + i, n // 2)
        query = jnp.concatenate(
            [
                jnp.where(low, msg[first + one, 0:TOKB].astype(F32), 0.0).astype(BF16)
                for one in range(2)
            ],
            axis=0,
        )
        acc = jnp.zeros((2 * TOKB, 128), F32)
        for c in range(rows // width):
            part = slice(c * width, (c + 1) * width)
            expo = jnp.exp2(dot_nt(query, keys[part, :]) * scale).astype(BF16)
            acc = acc + dot(expo, values[part, :])
        ctx = acc / acc[:, HEAD : HEAD + 1]
        for one in range(2):
            peer = first + one
            mine = ctx[one * TOKB : (one + 1) * TOKB]
            packed = jnp.where(low_half, mine[:half], swap_halves(mine[half:])).astype(BF16)

            @pl.when(peer != me)
            def _():
                outctx[peer] = packed
                remote(
                    outctx.at[peer], inctx.at[me], ctx_send.at[peer], ctx_recv.at[me], "sec", peer
                ).start()

            @pl.when(peer == me)
            def _():
                inctx[me] = packed

        return 0

    lax.fori_loop(0, n // 2, attend, 0)

    def collect(i, _):
        peer = lax.rem(me + n - i, n)
        remote(
            outctx.at[peer], inctx.at[peer], ctx_send.at[peer], ctx_recv.at[peer], "sec", peer
        ).wait()
        return 0

    lax.fori_loop(1, n, collect, 0)


def render_kernel(
    n,
    nd,
    ids,
    inctx,
    normed,
    cotan,
    out_hbm,
    vox_hbm,
    den_w,
    rays_hbm,
    depth_ref,
    grad_ref,
    ctx,
    mixed_ref,
    vox,
    dens,
    out_w,
    vox_w,
    rays,
    tau_out,
    tau_in,
    part_out,
    part_in,
    row_out,
    row_in,
    full_out,
    full_in,
    load_sem,
    tau_send,
    tau_recv,
    part_send,
    part_recv,
    row_send,
    row_recv,
    full_send,
    full_recv,
):
    me = lax.axis_index("sec")
    clip = lax.axis_index("dp")
    loads = [
        pltpu.make_async_copy(out_hbm, out_w, load_sem.at[0]),
        pltpu.make_async_copy(vox_hbm, vox_w, load_sem.at[1]),
        pltpu.make_async_copy(rays_hbm, rays, load_sem.at[2]),
    ]
    for load in loads:
        load.start()
    greet("sec", n)
    greet("dp", nd)
    half = TOKB // 2
    low = low_lanes(half)
    for t in range(HEADS // 2):
        even, odd = inctx[2 * t].astype(F32), inctx[2 * t + 1].astype(F32)
        lanes = slice(t * 128, (t + 1) * 128)
        ctx[0:half, lanes] = jnp.where(low, even, swap_halves(odd)).astype(BF16)
        ctx[half:TOKB, lanes] = jnp.where(low, swap_halves(even), odd).astype(BF16)
    loads[0].wait()
    mixed = (normed[...].astype(F32) + dot(ctx[...], out_w[...])).astype(BF16)
    mixed_ref[...] = mixed
    logit = dot(mixed, den_w[...])
    term = cotan[...].astype(F32) * jax.nn.sigmoid(logit)
    part = lax.dot_general(
        jnp.transpose(term)[:HEIGHTS],
        mixed.astype(F32),
        (((1,), (0,)), ((), ())),
        precision=lax.Precision.HIGHEST,
        preferred_element_type=F32,
    )
    for p in range(n):
        c, h = p // 2, p % 2
        part_out[p] = part[h * 8 : h * 8 + 8, c * 128 : (c + 1) * 128]
    pl.semaphore_wait(pltpu.get_barrier_semaphore(), n - 1 + nd - 1)

    def send_part(i, _):
        peer = lax.rem(me + i, n)
        remote(
            part_out.at[peer], part_in.at[me], part_send.at[peer], part_recv.at[me], "sec", peer
        ).start()
        return 0

    lax.fori_loop(1, n, send_part, 0)
    part_in[me] = part_out[me]

    density = LN2 * softplus2(LOG2E * logit)
    loads[1].wait()
    blocks = vox.shape[0]
    for pair in range(HEIGHTS // 2):
        two = dot(mixed_ref[...], vox_w[:, pair * 256 : (pair + 1) * 256])
        vox[:, pair * 16 : pair * 16 + 16, :] = jnp.concatenate(
            [two[:, :128].reshape(blocks, 8, 128), two[:, 128:].reshape(blocks, 8, 128)], axis=1
        ).astype(BF16)
        for one in range(2):
            h = pair * 2 + one
            dens[:, h * 8 : h * 8 + 8, :] = jnp.broadcast_to(
                density[:, h : h + 1], (TOKB, 128)
            ).reshape(blocks, 8, 128)
    loads[2].wait()
    bundles = rays.shape[0] // 128
    owned = bundles // n
    factor = LN2 * 4.0 / (n * KB * 128)

    def render(i, _):
        peer = lax.rem(me + i, n)
        for y in range(owned):
            bundle = peer * owned + y
            ray = rays[pl.ds(pl.multiple_of(bundle * 128, 128), 128), :]
            total = jnp.zeros((8, 128), F32)
            for j in range(KB):
                block = ids[bundle, j]
                score = dot_nt(vox[block], ray)
                value = softplus2(score * LOG2E) * dens[block]
                total = total + jnp.sum(value.reshape(16, 8, 128), axis=0)
            tau_out[peer, y : y + 1, :] = jnp.sum(total, axis=0, keepdims=True) * factor

        @pl.when(i < n)
        def _():
            remote(
                tau_out.at[peer], tau_in.at[me], tau_send.at[peer], tau_recv.at[me], "sec", peer
            ).start()

        @pl.when(i == n)
        def _():
            tau_in[me] = tau_out[me]

        return 0

    lax.fori_loop(1, 4, render, 0)

    def wait_part(i, _):
        peer = lax.rem(me + n - i, n)
        remote(
            part_out.at[peer], part_in.at[peer], part_send.at[peer], part_recv.at[peer], "sec", peer
        ).wait()
        return 0

    lax.fori_loop(1, n, wait_part, 0)
    row = part_in[0]
    for r in range(1, n):
        row = row + part_in[r]
    row_out[...] = row
    row_in[clip] = row

    def send_row(i, _):
        peer = lax.rem(clip + i, nd)
        remote(row_out, row_in.at[clip], row_send.at[peer], row_recv.at[clip], "dp", peer).start()
        return 0

    lax.fori_loop(1, nd, send_row, 0)
    lax.fori_loop(4, 9, render, 0)

    def wait_row(i, _):
        peer = lax.rem(clip + nd - i, nd)
        remote(row_out, row_in.at[peer], row_send.at[peer], row_recv.at[peer], "dp", peer).wait()
        return 0

    lax.fori_loop(1, nd, wait_row, 0)
    full = row_in[0]
    for r in range(1, nd):
        full = full + row_in[r]
    full_out[...] = full
    full_in[me] = full

    def send_full(i, _):
        peer = lax.rem(me + i, n)
        remote(full_out, full_in.at[me], full_send.at[peer], full_recv.at[me], "sec", peer).start()
        return 0

    lax.fori_loop(1, n, send_full, 0)
    lax.fori_loop(9, n + 1, render, 0)

    def finish(i, _):
        peer = lax.rem(me + n - i, n)
        remote(
            full_out, full_in.at[peer], full_send.at[peer], full_recv.at[peer], "sec", peer
        ).wait()
        remote(
            tau_out.at[peer], tau_in.at[peer], tau_send.at[peer], tau_recv.at[peer], "sec", peer
        ).wait()
        return 0

    lax.fori_loop(1, n, finish, 0)
    for p in range(n):
        c, h = p // 2, p % 2
        grad_ref[h * 8 : h * 8 + 8, c * 128 : (c + 1) * 128] = full_in[p]
    before = jnp.zeros(tau_in.shape[1:], F32)
    depth = jnp.zeros(tau_in.shape[1:], F32)
    for r in range(n):
        tau = tau_in[r]
        depth = depth + (r + 0.5) * jnp.exp(-before) * (1.0 - jnp.exp(-tau))
        before = before + tau
    depth_ref[...] = depth


def any_space():
    return pl.BlockSpec(memory_space=pl.ANY)


def vmem():
    return pl.BlockSpec(memory_space=pltpu.VMEM)


def dma(count):
    return pltpu.SemaphoreType.DMA((count,))


def params(number):
    return pltpu.CompilerParams(
        collective_id=number, has_side_effects=True, vmem_limit_bytes=VMEM_LIMIT
    )


def shards(
    range_features,
    conv_weight,
    cell_cycle,
    cell_token,
    in_weight,
    qkv_weight,
    out_weight,
    voxel_weight,
    density_weight,
    ray_embed,
    block_ids,
    density_cotangent,
):
    _, az_dev, beams, width = range_features.shape
    n, nd = lax.axis_size("sec"), lax.axis_size("dp")
    cells = az_dev * beams
    feats = range_features.reshape(cells, width)
    gid = (cell_cycle.reshape(az_dev, beams) * TOKB + cell_token).reshape(1, cells)
    message = (n, TOKB + TOKB // 2, 128)
    normed, msg = pl.pallas_call(
        functools.partial(encode_kernel, n, cells, beams),
        out_shape=(
            jax.ShapeDtypeStruct((TOKB, D), BF16),
            jax.ShapeDtypeStruct(message, BF16),
        ),
        in_specs=[any_space(), any_space(), vmem(), any_space(), any_space()],
        out_specs=(vmem(), vmem()),
        scratch_shapes=[
            pltpu.VMEM((cells + 2 * beams, width), BF16),
            pltpu.VMEM((cells, width), BF16),
            pltpu.VMEM((n, TOKB, width), BF16),
            pltpu.VMEM((n, TOKB, width), BF16),
            pltpu.VMEM((n, 8, TOKB), F32),
            pltpu.VMEM((n, 8, TOKB), F32),
            pltpu.VMEM(message, BF16),
            pltpu.VMEM(conv_weight.shape, BF16),
            pltpu.VMEM(in_weight.shape, BF16),
            pltpu.VMEM(qkv_weight.shape, BF16),
            dma(4),
            dma(2),
            dma(2),
            dma(n),
            dma(n),
            dma(n),
            dma(n),
            dma(n),
            dma(n),
        ],
        compiler_params=params(0),
        name="encode",
    )(feats, conv_weight, gid, in_weight, qkv_weight)
    context = (n, TOKB // 2, 128)
    ctx = pl.pallas_call(
        functools.partial(attention_kernel, n),
        out_shape=jax.ShapeDtypeStruct(context, BF16),
        in_specs=[vmem()],
        out_specs=vmem(),
        scratch_shapes=[
            pltpu.VMEM((n * TOKB, 128), BF16),
            pltpu.VMEM((n * TOKB, 128), BF16),
            pltpu.VMEM(context, BF16),
            dma(n),
            dma(n),
        ],
        compiler_params=params(1),
        name="attend",
    )(msg)
    bundles = ray_embed.shape[0] // 128
    owned = bundles // n
    depth, grad = pl.pallas_call(
        functools.partial(render_kernel, n, nd),
        out_shape=(
            jax.ShapeDtypeStruct((owned, 128), F32),
            jax.ShapeDtypeStruct((HEIGHTS, D), F32),
        ),
        in_specs=[
            pl.BlockSpec(memory_space=pltpu.SMEM),
            vmem(),
            vmem(),
            vmem(),
            any_space(),
            any_space(),
            vmem(),
            any_space(),
        ],
        out_specs=(vmem(), vmem()),
        scratch_shapes=[
            pltpu.VMEM((TOKB, D), BF16),
            pltpu.VMEM((TOKB, D), BF16),
            pltpu.VMEM((TOKB * HEIGHTS // 128, 128, EMB), BF16),
            pltpu.VMEM((TOKB * HEIGHTS // 128, 128, 128), F32),
            pltpu.VMEM(out_weight.shape, BF16),
            pltpu.VMEM(voxel_weight.shape, BF16),
            pltpu.VMEM(ray_embed.shape, BF16),
            pltpu.VMEM((n, owned, 128), F32),
            pltpu.VMEM((n, owned, 128), F32),
            pltpu.VMEM((n, 8, 128), F32),
            pltpu.VMEM((n, 8, 128), F32),
            pltpu.VMEM((8, 128), F32),
            pltpu.VMEM((nd, 8, 128), F32),
            pltpu.VMEM((8, 128), F32),
            pltpu.VMEM((n, 8, 128), F32),
            dma(3),
            dma(n),
            dma(n),
            dma(n),
            dma(n),
            dma(nd),
            dma(nd),
            dma(n),
            dma(n),
        ],
        compiler_params=params(2),
        name="render",
    )(
        block_ids[0],
        ctx,
        normed,
        density_cotangent[0],
        out_weight,
        voxel_weight,
        density_weight,
        ray_embed,
    )
    return depth.reshape(1, owned * 128), grad


def solution(mesh):
    placed = (
        P("dp", "sec", None, None),
        P(),
        P("sec", None, None),
        P("sec", None),
        P(),
        P(),
        P(),
        P(),
        P(),
        P(),
        P("sec", None, None),
        P("dp", "sec", None),
    )
    return jax.shard_map(
        shards, mesh=mesh, in_specs=placed, out_specs=(P("dp", "sec"), P()), check_vma=False
    )
```

time: 802 us -> 139 us (0.17)
  waiting for transfers between devices: 451 us -> 0 us
  local copies, waits for them, and re-layouts: 151 us -> 5.74 us
  Pallas kernels: 0 us -> 132 us
  matrix products: 112 us -> 0 us
  other arithmetic: 50.8 us -> 0.78 us
  starting transfers between devices: 17.7 us -> 0 us
  between operations: 14.8 us -> 0.67 us
    psum x1 -> x0, waiting for transfers between devices: 143 us -> none  [shards(): grad = lax.psum(part, ('sec', 'dp'))]
    all_gather x3 -> x0, waiting for transfers between devices: 140 us -> none  [the longest x1 66.8 us: shards(): keys = lax.all_gather(key_value[:, :D], 'sec', axis=0, tiled=True)]
    pallas_call x0 -> x3, Pallas kernels: none -> 132 us  [the longest x1 68 us: shards(): pl.pallas_call(functools.partial(encode_kernel, n, cells, beams), out_sha...]
    dot_general x20 -> x0, matrix products: 112 us -> none  [the longest x8 35.4 us: one_bundle(): lax.dot_general(rays_here, chosen, (((1,), (1,)), ((), ())), preferred_el...]
    all_to_all x2 -> x0, waiting for transfers between devices: 89.2 us -> none  [the longest x1 89.2 us: shards(): lax.all_to_all(outbox.reshape(n_sec, cap, width), 'sec', split_axis=0, co...]
    unnamed x6 -> x0, waiting for transfers between devices: 78.8 us -> none
    gather x17 -> x0, local copies, waits for them, and re-layouts: 54.9 us -> none  [the longest x1 33 us: shards(): place = jnp.take_along_axis(running, cycle[:, None], axis=1)[:, 0] - 1]
    reduce_sum x9 -> x0, other arithmetic: 40.9 us -> none  [the longest x8 38.8 us: one_bundle(): return jnp.sum(jax.nn.softplus(scores) * dens[None, :], axis=-1)]
  transfers between devices with their start and end apart: 9 -> 0, of which waited for: 6 -> 0; matrix products, arithmetic and copies ran while one was open for 17% -> 0% of each run, Pallas kernels for 0% -> 0%
where the time goes in v1:
time: 139 us
  Pallas kernels  132 us (95%)
  local copies, waits for them, and re-layouts  5.74 us (4%)
    pallas_call x1, Pallas kernels, shards(): pl.pallas_call(functools.partial(encode_kernel, n, cells, beams), out_sha...  68 us
    pallas_call x1, Pallas kernels, shards(): pl.pallas_call(functools.partial(attention_kernel, n), out_shape=jax.Shap...  35.2 us
    pallas_call x1, Pallas kernels, shards(): pl.pallas_call(functools.partial(render_kernel, n, nd), out_shape=(jax.Sh...  28.3 us
    unnamed x11, local copies, waits for them, and re-layouts  5.04 us

profile of v1, /device:TPU:1, one launch (start us, length us, event | category | flops | bytes accessed | tf_op | source)
XLA Modules:
  0.0 138.7 jit_solution(10074420799513663765)
XLA Ops:
  0.6 0.8 bitcast_add_fusion
  1.4 0.7 reshape.17.gid_ref
  2.1 0.0 copy-start
  2.1 0.0 copy-start.2
  2.1 0.0 copy-start.1
  2.1 68.0 %encode.1 = (bf16[256,1024]{1,0:T(8,128)(2,1)}, bf16[16,384,128]{2,1,0:T(8,128)(2,1)}) custom-call(bf16[4096,256]{1,0:T(8,128)(2,1)} %bitcast.7, bf16[3,256,256]{2,1,0:T(8,128)(2,1)} %conv_hbm.1, s32[1,4096]{1,0:T(1,128)} %reshape.17.gid_ref, bf16[256,1024]{1,0:T(8,128)(2,1)} %in_hbm.1, bf16[1024,3072]{1,0:T(8,128)(2,1)} %qkv_hbm.1), custom_call_target="tpu_custom_call" | custom-call | tf_op jit(solution)/shard_map/encode/pallas_call | solution.py:594
  70.1 35.2 %attend.1.inctx = bf16[16,128,128]{2,1,0:T(8,128)(2,1)} custom-call(bf16[16,384,128]{2,1,0:T(8,128)(2,1)} %get-tuple-element.6.msg), custom_call_target="tpu_custom_call" | custom-call | tf_op jit(solution)/shard_map/attend/pallas_call | solution.py:627
  105.3 0.0 copy-done
  105.3 0.8 copy.17.den_w
  106.1 0.0 copy-done.2
  106.1 0.7 copy.14
  106.9 0.0 copy-done.1
  106.9 0.7 copy.16
  107.6 28.3 %render.1 = (f32[8,128]{1,0:T(8,128)}, f32[16,1024]{1,0:T(8,128)}) custom-call(s32[128,4]{1,0:T(8,128)} %bitcast.8, bf16[16,128,128]{2,1,0:T(8,128)(2,1)} %attend.1.inctx, bf16[256,1024]{1,0:T(8,128)(2,1)} %get-tuple-element.7.normed, bf16[256,16]{1,0:T(8,128)(2,1)} %bitcast.9, bf16[1024,1024]{1,0:T(8,128)(2,1)} %out_hbm.1, bf16[1024,2048]{1,0:T(8,128)(2,1)} %vox_hbm.1, ...), custom_call_target="tpu_custom_call" | custom-call | tf_op jit(solution)/shard_map/render/pallas_call | solution.py:644
  135.9 1.3 copy.20
  137.2 1.5 %copy.21 = f32[16,1024]{1,0:T(8,128)} copy(f32[16,1024]{1,0:T(8,128)} %get-tuple-element.13) | data formatting | bytes 131072
Async XLA Ops:
  2.1 103.2 %copy-start = (bf16[1024,16]{0,1:T(8,128)(2,1)S(1)}, bf16[1024,16]{0,1:T(8,128)(2,1)}, u32[]{:S(2)}) copy-start(bf16[1024,16]{0,1:T(8,128)(2,1)} %param.20) | copy-start | bytes 98308
  2.1 104.0 %copy-start.2 = (s32[1,128,4]{1,2,0:T(4,128)S(1)}, s32[1,128,4]{1,2,0:T(4,128)}, u32[]{:S(2)}) copy-start(s32[1,128,4]{1,2,0:T(4,128)} %param.22) | copy-start | bytes 6148
  2.1 104.8 %copy-start.1 = (bf16[1,256,16]{1,2,0:T(8,128)(2,1)S(1)}, bf16[1,256,16]{1,2,0:T(8,128)(2,1)}, u32[]{:S(2)}) copy-start(bf16[1,256,16]{1,2,0:T(8,128)(2,1)} %param.23) | copy-start | bytes 24580

commit v2 on v0

v2 whole, which is shorter than its diff:
```python
import functools
import math

import jax
import jax.numpy as jnp
from jax import lax
from jax.experimental import pallas as pl
from jax.experimental.pallas import tpu as pltpu
from jax.sharding import PartitionSpec as P

D = 1024
HEADS = 16
HEAD = 64
EMB = 128
KB = 4
TOKB = 256
HEIGHTS = 16
MESH = pl.DeviceIdType.MESH
BF16 = jnp.bfloat16
F32 = jnp.float32
VMEM_LIMIT = 60 * 1024 * 1024
LOG2E = math.log2(math.e)


def dot(a, b):
    return jnp.dot(a, b, preferred_element_type=F32)


def dot_nt(a, b):
    return lax.dot_general(a, b, (((1,), (1,)), ((), ())), preferred_element_type=F32)


def greet(axis, n):
    me = lax.axis_index(axis)
    barrier = pltpu.get_barrier_semaphore()

    def hello(i, _):
        pl.semaphore_signal(
            barrier, inc=1, device_id={axis: lax.rem(me + i, n)}, device_id_type=MESH
        )
        return 0

    lax.fori_loop(1, n, hello, 0)


def remote(src, dst, send_sem, recv_sem, axis, peer):
    return pltpu.make_async_remote_copy(
        src_ref=src,
        dst_ref=dst,
        send_sem=send_sem,
        recv_sem=recv_sem,
        device_id={axis: peer},
        device_id_type=MESH,
    )


def swap_halves(x):
    return pltpu.roll(x, HEAD, 1)


def low_lanes(rows):
    return lax.broadcasted_iota(jnp.int32, (rows, 128), 1) < HEAD


def each_peer(n, me, step):
    def body(i, _):
        step(lax.rem(me + n - i, n))
        return 0

    lax.fori_loop(1, n, body, 0)


def gelu(x):
    inner = math.sqrt(2.0 / math.pi) * (x + 0.044715 * (x * x * x))
    return x * (0.5 * (1.0 + jnp.tanh(inner)))


def softplus(x):
    return jnp.maximum(x, lax.log(1.0 + jnp.exp2(jnp.minimum(x, 80.0) * LOG2E)))


def forecast_kernel(
    n,
    nd,
    cells,
    beams,
    ids,
    cyc_ref,
    tok_ref,
    den_t,
    cot_t,
    feats,
    conv_hbm,
    in_hbm,
    qkv_hbm,
    out_hbm,
    vox_hbm,
    rays_hbm,
    tau_in,
    full_in,
    gid_ref,
    padded,
    enc,
    outbox,
    inbox,
    cnt_out,
    cnt_in,
    outmsg,
    inmsg,
    normed_ref,
    queries,
    values,
    accs,
    outctx,
    inctx,
    mixed_ref,
    vox,
    dens,
    tau_out,
    part_out,
    part_in,
    row_out,
    row_in,
    full_out,
    conv_w,
    in_w,
    qkv_w,
    out_w,
    vox_w,
    rays,
    load_sem,
    halo_send,
    halo_recv,
    box_send,
    box_recv,
    cnt_send,
    cnt_recv,
    msg_send,
    msg_recv,
    ctx_send,
    ctx_recv,
    tau_send,
    tau_recv,
    part_send,
    part_recv,
    row_send,
    row_recv,
    full_send,
    full_recv,
):
    me = lax.axis_index("sec")
    clip = lax.axis_index("dp")
    greet("sec", n)
    greet("dp", nd)
    loads = [
        pltpu.make_async_copy(feats, padded.at[pl.ds(beams, cells)], load_sem.at[0]),
        pltpu.make_async_copy(conv_hbm, conv_w, load_sem.at[1]),
        pltpu.make_async_copy(in_hbm, in_w, load_sem.at[2]),
        pltpu.make_async_copy(qkv_hbm, qkv_w, load_sem.at[3]),
        pltpu.make_async_copy(out_hbm, out_w, load_sem.at[4]),
        pltpu.make_async_copy(vox_hbm, vox_w, load_sem.at[5]),
        pltpu.make_async_copy(rays_hbm, rays, load_sem.at[6]),
    ]
    for load in loads:
        load.start()

    gid = cyc_ref[...] * TOKB + tok_ref[...]
    for p in range(cells // 128):
        gid_ref[0:1, p * 128 : (p + 1) * 128] = jnp.concatenate(
            [gid[2 * p : 2 * p + 1, :], gid[2 * p + 1 : 2 * p + 2, :]], axis=1
        )
    row = gid_ref[...]
    tok_hot = jnp.where(
        lax.broadcasted_iota(jnp.int32, (TOKB, cells), 0) == (row & (TOKB - 1)), 1.0, 0.0
    ).astype(BF16)
    cyc_hot = jnp.where(
        lax.broadcasted_iota(jnp.int32, (n, cells), 0) == (row >> 8), 1.0, 0.0
    ).astype(BF16)
    hist = dot_nt(cyc_hot, tok_hot)
    for r in range(n):
        cnt_out[r] = jnp.broadcast_to(hist[r : r + 1, :], (8, TOKB))

    pl.semaphore_wait(pltpu.get_barrier_semaphore(), n - 1 + nd - 1)
    halos = [
        remote(
            feats.at[pl.ds(cells - beams, beams)],
            padded.at[pl.ds(0, beams)],
            halo_send.at[0],
            halo_recv.at[0],
            "sec",
            lax.rem(me + 1, n),
        ),
        remote(
            feats.at[pl.ds(0, beams)],
            padded.at[pl.ds(beams + cells, beams)],
            halo_send.at[1],
            halo_recv.at[1],
            "sec",
            lax.rem(me + n - 1, n),
        ),
    ]
    for halo in halos:
        halo.start()

    rows = 16 * beams
    chunks = cells // rows

    def encode_chunk(c):
        base = pl.multiple_of(c * rows, rows)
        total = jnp.zeros((rows, enc.shape[1]), F32)
        for k in range(3):
            total = total + dot(padded[pl.ds(base + k * beams, rows), :], conv_w[k])
        own = padded[pl.ds(base + beams, rows), :].astype(F32)
        enc[pl.ds(base, rows), :] = (own + gelu(total)).astype(BF16)

    loads[0].wait()
    loads[1].wait()

    def chunk(i, _):
        @pl.when(i == chunks - 2)
        def _():
            for halo in halos:
                halo.wait()

        encode_chunk(lax.rem(i + 1, chunks))
        return 0

    lax.fori_loop(0, chunks, chunk, 0)

    def pool(i, _):
        first = 2 * lax.rem(me // 2 + 1 + i, n // 2)
        hot = jnp.where(
            lax.broadcasted_iota(jnp.int32, (2 * TOKB, cells), 0) == (gid_ref[...] - first * TOKB),
            1.0,
            0.0,
        ).astype(BF16)
        both = dot(hot, enc[...]).astype(BF16)
        for one in range(2):
            peer = first + one
            part = both[one * TOKB : (one + 1) * TOKB]

            @pl.when(peer != me)
            def _():
                outbox[peer] = part
                remote(
                    outbox.at[peer], inbox.at[me], box_send.at[peer], box_recv.at[me], "sec", peer
                ).start()
                remote(
                    cnt_out.at[peer], cnt_in.at[me], cnt_send.at[peer], cnt_recv.at[me], "sec", peer
                ).start()

            @pl.when(peer == me)
            def _():
                inbox[me] = part
                cnt_in[me] = cnt_out[me]

        return 0

    lax.fori_loop(0, n // 2, pool, 0)

    last = values.shape[1] - HEAD
    ones = jnp.where(
        lax.broadcasted_iota(jnp.int32, (last, values.shape[2]), 0) == 0, 1.0, 0.0
    ).astype(BF16)
    for c in range(values.shape[0]):
        values[c, HEAD:, :] = ones
    accs[...] = jnp.zeros_like(accs)

    def arrive(peer):
        remote(
            cnt_out.at[peer], cnt_in.at[peer], cnt_send.at[peer], cnt_recv.at[peer], "sec", peer
        ).wait()
        remote(
            outbox.at[peer], inbox.at[peer], box_send.at[peer], box_recv.at[peer], "sec", peer
        ).wait()

    each_peer(n, me, arrive)
    loads[2].wait()
    loads[3].wait()
    sums = inbox[0].astype(F32)
    counts = cnt_in[0]
    for r in range(1, n):
        sums = sums + inbox[r].astype(F32)
        counts = counts + cnt_in[r]
    root = jnp.sqrt(jnp.transpose(counts)[:, 0:1] + 1.0)
    pooled = (sums / root).astype(BF16)
    lifted = dot(pooled, in_w[...])
    normed_ref[...] = (
        lifted * lax.rsqrt(jnp.mean(lifted * lifted, axis=-1, keepdims=True) + 1e-06)
    ).astype(BF16)

    low = low_lanes(TOKB)
    half = TOKB // 2
    planes = HEADS // 4

    def project(i, _):
        group = lax.rem(me // 4 + i, planes)
        column = group * (4 * HEAD)
        q4, k4, v4 = (
            dot(
                normed_ref[...],
                qkv_w[:, pl.ds(pl.multiple_of(part * D + column, 4 * HEAD), 4 * HEAD)],
            )
            for part in range(3)
        )
        q4 = q4 * HEAD ** (-0.5)
        vt = jnp.transpose(v4).astype(BF16)
        for one in range(4):
            peer = group * 4 + one
            lanes = slice(one // 2 * 128, one // 2 * 128 + 128)
            q, k = q4[:, lanes], k4[:, lanes]
            if one % 2 == 0:
                packed = jnp.where(low, q, swap_halves(k))
            else:
                packed = jnp.where(low, swap_halves(q), k)
            outmsg[peer, 0:TOKB] = packed.astype(BF16)
            mine = vt[one * HEAD : (one + 1) * HEAD]
            outmsg[peer, TOKB : TOKB + HEAD] = mine[:, :half]
            outmsg[peer, TOKB + HEAD : TOKB + 2 * HEAD] = mine[:, half:]

            @pl.when(peer != me)
            def _():
                remote(
                    outmsg.at[peer], inmsg.at[me], msg_send.at[peer], msg_recv.at[me], "sec", peer
                ).start()

            @pl.when(peer == me)
            def _():
                inmsg[me] = outmsg[me]

        return 0

    lax.fori_loop(0, planes, project, 0)

    def meet(q, k):
        acc = accs[q]
        for c in range(2):
            first = k * 4 + 2 * c
            key = jnp.concatenate([inmsg[first, 0:TOKB], inmsg[first + 1, 0:TOKB]], axis=0)
            expo = jnp.exp2(dot_nt(key, queries[q]) * LOG2E).astype(BF16)
            acc = acc + dot(values[k * 2 + c], expo)
        accs[q] = acc

    def stage(i, _):
        plane = lax.rem(me // 4 + planes - i, planes)
        for one in range(4):
            peer = plane * 4 + one

            @pl.when(peer != me)
            def _():
                remote(
                    outmsg.at[peer],
                    inmsg.at[peer],
                    msg_send.at[peer],
                    msg_recv.at[peer],
                    "sec",
                    peer,
                ).wait_recv()

            qk = inmsg[peer, 0:TOKB].astype(F32)
            queries[plane, one * TOKB : (one + 1) * TOKB] = jnp.where(
                low, 0.0, swap_halves(qk)
            ).astype(BF16)
            chunk = plane * 2 + one // 2
            base = one % 2 * TOKB
            values[chunk, 0:HEAD, base : base + half] = inmsg[peer, TOKB : TOKB + HEAD]
            values[chunk, 0:HEAD, base + half : base + TOKB] = inmsg[
                peer, TOKB + HEAD : TOKB + 2 * HEAD
            ]

        def pair(t, _):
            fresh = t >= i
            back_q = jnp.where(fresh, i, t)
            back_k = jnp.where(fresh, t - i, i)
            q = lax.rem(me // 4 + planes - back_q, planes)
            meet(q, lax.rem(me // 4 + planes - back_k, planes))

            @pl.when((i == planes - 1) & ((t < i) | (t == 2 * i)))
            def _():
                acc = accs[q]
                ctx = (acc[:HEAD] / acc[HEAD : HEAD + 1]).astype(BF16)
                for one in range(4):
                    peer = q * 4 + one
                    mine = ctx[:, one * TOKB : (one + 1) * TOKB]

                    @pl.when(peer != me)
                    def _():
                        outctx[peer] = mine
                        remote(
                            outctx.at[peer],
                            inctx.at[me],
                            ctx_send.at[peer],
                            ctx_recv.at[me],
                            "sec",
                            peer,
                        ).start()

                    @pl.when(peer == me)
                    def _():
                        inctx[me] = mine

            return 0

        lax.fori_loop(0, 2 * i + 1, pair, 0)
        return 0

    lax.fori_loop(0, planes, stage, 0)

    def context(peer):
        remote(
            outmsg.at[peer], inmsg.at[peer], msg_send.at[peer], msg_recv.at[peer], "sec", peer
        ).wait_send()
        remote(
            outctx.at[peer], inctx.at[peer], ctx_send.at[peer], ctx_recv.at[peer], "sec", peer
        ).wait()

    each_peer(n, me, context)
    for load in loads[4:]:
        load.wait()

    ctx = jnp.transpose(inctx[...].reshape(D, TOKB))
    mixed = (normed_ref[...].astype(F32) + dot(ctx, out_w[...])).astype(BF16)
    mixed_ref[...] = mixed
    term = cot_t[...].astype(F32) * jax.nn.sigmoid(dot_nt(den_t[...], mixed))
    part = lax.dot_general(
        term,
        mixed.astype(F32),
        (((1,), (0,)), ((), ())),
        precision=lax.Precision.HIGHEST,
        preferred_element_type=F32,
    )
    for p in range(n):
        c, h = p // 2, p % 2
        part_out[p] = part[h * 8 : h * 8 + 8, c * 128 : (c + 1) * 128]

    def send_part(peer):
        remote(
            part_out.at[peer], part_in.at[me], part_send.at[peer], part_recv.at[me], "sec", peer
        ).start()

    each_peer(n, me, send_part)
    part_in[me] = part_out[me]

    density = softplus(dot_nt(mixed, den_t[...]))
    blocks = vox.shape[0]
    for pair in range(HEIGHTS // 2):
        two = dot(mixed_ref[...], vox_w[:, pair * 256 : (pair + 1) * 256])
        vox[:, pair * 16 : pair * 16 + 16, :] = jnp.concatenate(
            [two[:, :128].reshape(blocks, 8, 128), two[:, 128:].reshape(blocks, 8, 128)], axis=1
        ).astype(BF16)
        for one in range(2):
            h = pair * 2 + one
            dens[:, h * 8 : h * 8 + 8, :] = jnp.broadcast_to(
                density[:, h : h + 1], (TOKB, 128)
            ).reshape(blocks, 8, 128)
    bundles = rays.shape[0] // 128
    owned = bundles // n
    factor = 4.0 / (n * KB * 128)

    def render(i, _):
        peer = lax.rem(me + i, n)
        for y in range(owned):
            bundle = peer * owned + y
            ray = rays[pl.ds(pl.multiple_of(bundle * 128, 128), 128), :]
            picks = [ids[j, bundle] for j in range(KB)]
            score = dot_nt(jnp.concatenate([vox[b] for b in picks], axis=0), ray)
            total = jnp.zeros((8, 128), F32)
            for j in range(KB):
                value = softplus(score[j * 128 : (j + 1) * 128]) * dens[picks[j]]
                total = total + jnp.sum(value.reshape(16, 8, 128), axis=0)
            tau_out[peer, y : y + 1, :] = jnp.sum(total, axis=0, keepdims=True) * factor

        @pl.when(i < n)
        def _():
            remote(
                tau_out.at[peer], tau_in.at[me], tau_send.at[peer], tau_recv.at[me], "sec", peer
            ).start()

        @pl.when(i == n)
        def _():
            tau_in[me] = tau_out[me]

        @pl.when(i == 3)
        def _():
            def wait_part(peer):
                remote(
                    part_out.at[peer],
                    part_in.at[peer],
                    part_send.at[peer],
                    part_recv.at[peer],
                    "sec",
                    peer,
                ).wait()

            each_peer(n, me, wait_part)
            row = part_in[0]
            for r in range(1, n):
                row = row + part_in[r]
            row_out[...] = row
            row_in[clip] = row

            def send_row(peer):
                remote(
                    row_out, row_in.at[clip], row_send.at[peer], row_recv.at[clip], "dp", peer
                ).start()

            each_peer(nd, clip, send_row)

        @pl.when(i == 8)
        def _():
            def wait_row(peer):
                remote(
                    row_out, row_in.at[peer], row_send.at[peer], row_recv.at[peer], "dp", peer
                ).wait()

            each_peer(nd, clip, wait_row)
            full = row_in[0]
            for r in range(1, nd):
                full = full + row_in[r]
            full_out[...] = full
            full_in[me] = full

            def send_full(peer):
                remote(
                    full_out, full_in.at[me], full_send.at[peer], full_recv.at[me], "sec", peer
                ).start()

            each_peer(n, me, send_full)

        return 0

    lax.fori_loop(1, n + 1, render, 0)

    def finish(peer):
        remote(
            full_out, full_in.at[peer], full_send.at[peer], full_recv.at[peer], "sec", peer
        ).wait()
        remote(
            tau_out.at[peer], tau_in.at[peer], tau_send.at[peer], tau_recv.at[peer], "sec", peer
        ).wait()

    each_peer(n, me, finish)


def finish_kernel(n, tau_ref, full_ref, depth_ref, grad_ref):
    for p in range(n):
        c, h = p // 2, p % 2
        grad_ref[h * 8 : h * 8 + 8, c * 128 : (c + 1) * 128] = full_ref[p]
    before = jnp.zeros(tau_ref.shape[1:], F32)
    depth = jnp.zeros(tau_ref.shape[1:], F32)
    for r in range(n):
        tau = tau_ref[r]
        depth = depth + (r + 0.5) * jnp.exp(-before) * (1.0 - jnp.exp(-tau))
        before = before + tau
    depth_ref[...] = depth


def any_space():
    return pl.BlockSpec(memory_space=pl.ANY)


def vmem():
    return pl.BlockSpec(memory_space=pltpu.VMEM)


def dma(count):
    return pltpu.SemaphoreType.DMA((count,))


def shards(
    range_features,
    conv_weight,
    cell_cycle,
    cell_token,
    in_weight,
    qkv_weight,
    out_weight,
    voxel_weight,
    density_weight,
    ray_embed,
    block_ids,
    density_cotangent,
):
    _, az_dev, beams, width = range_features.shape
    n, nd = lax.axis_size("sec"), lax.axis_size("dp")
    cells = az_dev * beams
    bundles = ray_embed.shape[0] // 128
    owned = bundles // n
    blocks = TOKB * HEIGHTS // 128
    message = (n, TOKB + TOKB // 2, 128)
    tau, full = pl.pallas_call(
        functools.partial(forecast_kernel, n, nd, cells, beams),
        out_shape=(
            jax.ShapeDtypeStruct((n, owned, 128), F32),
            jax.ShapeDtypeStruct((n, 8, 128), F32),
        ),
        in_specs=[pl.BlockSpec(memory_space=pltpu.SMEM)] + [vmem()] * 4 + [any_space()] * 7,
        out_specs=(vmem(), vmem()),
        scratch_shapes=[
            pltpu.VMEM((1, cells), jnp.int32),
            pltpu.VMEM((cells + 2 * beams, width), BF16),
            pltpu.VMEM((cells, width), BF16),
            pltpu.VMEM((n, TOKB, width), BF16),
            pltpu.VMEM((n, TOKB, width), BF16),
            pltpu.VMEM((n, 8, TOKB), F32),
            pltpu.VMEM((n, 8, TOKB), F32),
            pltpu.VMEM(message, BF16),
            pltpu.VMEM(message, BF16),
            pltpu.VMEM((TOKB, D), BF16),
            pltpu.VMEM((n // 4, 4 * TOKB, 128), BF16),
            pltpu.VMEM((n // 2, HEAD + 16, 2 * TOKB), BF16),
            pltpu.VMEM((n // 4, HEAD + 16, 4 * TOKB), F32),
            pltpu.VMEM((n, HEAD, TOKB), BF16),
            pltpu.VMEM((n, HEAD, TOKB), BF16),
            pltpu.VMEM((TOKB, D), BF16),
            pltpu.VMEM((blocks, 128, EMB), BF16),
            pltpu.VMEM((blocks, 128, 128), F32),
            pltpu.VMEM((n, owned, 128), F32),
            pltpu.VMEM((n, 8, 128), F32),
            pltpu.VMEM((n, 8, 128), F32),
            pltpu.VMEM((8, 128), F32),
            pltpu.VMEM((nd, 8, 128), F32),
            pltpu.VMEM((8, 128), F32),
            pltpu.VMEM(conv_weight.shape, BF16),
            pltpu.VMEM(in_weight.shape, BF16),
            pltpu.VMEM(qkv_weight.shape, BF16),
            pltpu.VMEM(out_weight.shape, BF16),
            pltpu.VMEM(voxel_weight.shape, BF16),
            pltpu.VMEM(ray_embed.shape, BF16),
            dma(7),
            dma(2),
            dma(2),
            dma(n),
            dma(n),
            dma(n),
            dma(n),
            dma(n),
            dma(n),
            dma(n),
            dma(n),
            dma(n),
            dma(n),
            dma(n),
            dma(n),
            dma(nd),
            dma(nd),
            dma(n),
            dma(n),
        ],
        compiler_params=pltpu.CompilerParams(
            collective_id=0, has_side_effects=True, vmem_limit_bytes=VMEM_LIMIT
        ),
        name="forecast",
    )(
        block_ids[0].T,
        cell_cycle.reshape(az_dev, beams),
        cell_token,
        density_weight.T,
        density_cotangent[0].T,
        range_features.reshape(cells, width),
        conv_weight,
        in_weight,
        qkv_weight,
        out_weight,
        voxel_weight,
        ray_embed,
    )
    depth, grad = pl.pallas_call(
        functools.partial(finish_kernel, n),
        out_shape=(
            jax.ShapeDtypeStruct((owned, 128), F32),
            jax.ShapeDtypeStruct((HEIGHTS, D), F32),
        ),
        in_specs=[vmem(), vmem()],
        out_specs=(vmem(), vmem()),
        name="finish",
    )(tau, full)
    return depth.reshape(1, owned * 128), grad


def solution(mesh):
    placed = (
        P("dp", "sec", None, None),
        P(),
        P("sec", None, None),
        P("sec", None),
        P(),
        P(),
        P(),
        P(),
        P(),
        P(),
        P("sec", None, None),
        P("dp", "sec", None),
    )
    return jax.shard_map(
        shards, mesh=mesh, in_specs=placed, out_specs=(P("dp", "sec"), P()), check_vma=False
    )
```

time: 802 us -> 114 us (0.14)
  waiting for transfers between devices: 451 us -> 0 us
  local copies, waits for them, and re-layouts: 151 us -> 0 us
  Pallas kernels: 0 us -> 113 us
  matrix products: 112 us -> 0 us
  other arithmetic: 50.8 us -> 0 us
  starting transfers between devices: 17.7 us -> 0 us
  between operations: 14.8 us -> 0.64 us
    psum x1 -> x0, waiting for transfers between devices: 143 us -> none  [shards(): grad = lax.psum(part, ('sec', 'dp'))]
    all_gather x3 -> x0, waiting for transfers between devices: 140 us -> none  [the longest x1 66.8 us: shards(): keys = lax.all_gather(key_value[:, :D], 'sec', axis=0, tiled=True)]
    pallas_call x0 -> x2, Pallas kernels: none -> 113 us  [the longest x1 112 us: shards(): pl.pallas_call(functools.partial(forecast_kernel, n, nd, cells, beams), o...]
    dot_general x20 -> x0, matrix products: 112 us -> none  [the longest x8 35.4 us: one_bundle(): lax.dot_general(rays_here, chosen, (((1,), (1,)), ((), ())), preferred_el...]
    all_to_all x2 -> x0, waiting for transfers between devices: 89.2 us -> none  [the longest x1 89.2 us: shards(): lax.all_to_all(outbox.reshape(n_sec, cap, width), 'sec', split_axis=0, co...]
    unnamed x6 -> x0, waiting for transfers between devices: 78.8 us -> none
    gather x17 -> x0, local copies, waits for them, and re-layouts: 54.9 us -> none  [the longest x1 33 us: shards(): place = jnp.take_along_axis(running, cycle[:, None], axis=1)[:, 0] - 1]
    reduce_sum x9 -> x0, other arithmetic: 40.9 us -> none  [the longest x8 38.8 us: one_bundle(): return jnp.sum(jax.nn.softplus(scores) * dens[None, :], axis=-1)]
  transfers between devices with their start and end apart: 9 -> 0, of which waited for: 6 -> 0; matrix products, arithmetic and copies ran while one was open for 17% -> 0% of each run, Pallas kernels for 0% -> 0%
where the time goes in v2:
time: 114 us
  Pallas kernels  113 us (99%)
    pallas_call x1, Pallas kernels, shards(): pl.pallas_call(functools.partial(forecast_kernel, n, nd, cells, beams), o...  112 us

profile of v2, /device:TPU:1, one launch (start us, length us, event | category | flops | bytes accessed | tf_op | source)
XLA Modules:
  0.0 113.7 jit_solution(1014139826888016206)
XLA Ops:
  0.6 111.6 %forecast.1 = (f32[16,8,128]{2,1,0:T(8,128)}, f32[16,8,128]{2,1,0:T(8,128)}) custom-call(s32[4,128]{1,0:T(4,128)} %bitcast.14, s32[64,64]{1,0:T(8,128)} %bitcast.11, s32[64,64]{1,0:T(8,128)} %tok_ref.1, bf16[16,1024]{1,0:T(8,128)(2,1)} %bitcast.12, bf16[16,256]{1,0:T(8,128)(2,1)} %bitcast.13, bf16[4096,256]{1,0:T(8,128)(2,1)} %bitcast.10, ...), custom_call_target="tpu_custom_call" | custom-call | tf_op jit(solution)/shard_map/forecast/pallas_call | solution.py:591
  112.2 1.5 %finish.1 = (f32[8,128]{1,0:T(8,128)}, f32[16,1024]{1,0:T(8,128)}) custom-call(f32[16,8,128]{2,1,0:T(8,128)} %get-tuple-element.6.tau_ref, f32[16,8,128]{2,1,0:T(8,128)} %get-tuple-element.7.full_ref), custom_call_target="tpu_custom_call" | custom-call | tf_op jit(solution)/shard_map/finish/pallas_call | solution.py:668

commit v3 on v2

--- a/solution.py
+++ b/solution.py
@@ -60,6 +60,37 @@
 
 def low_lanes(rows):
     return lax.broadcasted_iota(jnp.int32, (rows, 128), 1) < HEAD
+
+
+def pick(i, choices):
+    chosen = jnp.int32(choices[0])
+    for k, choice in enumerate(choices[1:]):
+        chosen = jnp.where(i == k + 1, choice, chosen)
+    return chosen
+
+
+def moved(me, dz, dy):
+    return lax.rem(me // 4 + dz + 4, 4) * 4 + lax.rem(me + dy + 4, 4)
+
+
+ORDER = (
+    ((1, 2), (-1, 2)),
+    ((2, 1), (2, -1)),
+    ((1, 1), (-1, -1)),
+    ((1, -1), (-1, 1)),
+    ((2, 0), (0, 2)),
+    ((2, 2), (1, 0)),
+    ((-1, 0), (0, 1)),
+    ((0, -1), (0, 0)),
+)
+PLANES = ((1, -1), (2, 0))
+GROUPS = (
+    ((1, 1), (-1, -1), (1, -1), (-1, 1)),
+    ((1, 2), (-1, 2), (2, 1), (2, -1)),
+    ((2, 2), (2, 0), (0, 2), (0, 0)),
+    ((1, 0), (-1, 0), (0, 1), (0, -1)),
+)
+WINDOW = 4
 
 
 def each_peer(n, me, step):
@@ -101,14 +132,19 @@
     gid_ref,
     padded,
     enc,
-    outbox,
-    inbox,
+    out_y,
+    in_y,
+    out_z,
+    in_z,
+    mid_out,
+    mid_in,
     cnt_out,
     cnt_in,
     outmsg,
     inmsg,
     normed_ref,
     queries,
+    keys,
     values,
     accs,
     outctx,
@@ -133,6 +169,8 @@
     halo_recv,
     box_send,
     box_recv,
+    mid_send,
+    mid_recv,
     cnt_send,
     cnt_recv,
     msg_send,
@@ -161,25 +199,13 @@
         pltpu.make_async_copy(vox_hbm, vox_w, load_sem.at[5]),
         pltpu.make_async_copy(rays_hbm, rays, load_sem.at[6]),
     ]
-    for load in loads:
+    for load in loads[:2]:
         load.start()
-
     gid = cyc_ref[...] * TOKB + tok_ref[...]
     for p in range(cells // 128):
         gid_ref[0:1, p * 128 : (p + 1) * 128] = jnp.concatenate(
             [gid[2 * p : 2 * p + 1, :], gid[2 * p + 1 : 2 * p + 2, :]], axis=1
         )
-    row = gid_ref[...]
-    tok_hot = jnp.where(
-        lax.broadcasted_iota(jnp.int32, (TOKB, cells), 0) == (row & (TOKB - 1)), 1.0, 0.0
-    ).astype(BF16)
-    cyc_hot = jnp.where(
-        lax.broadcasted_iota(jnp.int32, (n, cells), 0) == (row >> 8), 1.0, 0.0
-    ).astype(BF16)
-    hist = dot_nt(cyc_hot, tok_hot)
-    for r in range(n):
-        cnt_out[r] = jnp.broadcast_to(hist[r : r + 1, :], (8, TOKB))
-
     pl.semaphore_wait(pltpu.get_barrier_semaphore(), n - 1 + nd - 1)
     halos = [
         remote(
@@ -215,6 +241,8 @@
 
     loads[0].wait()
     loads[1].wait()
+    for load in loads[2:]:
+        load.start()
 
     def chunk(i, _):
         @pl.when(i == chunks - 2)
@@ -227,36 +255,112 @@
 
     lax.fori_loop(0, chunks, chunk, 0)
 
+    mz, my = me // 4, lax.rem(me, 4)
+    wide = enc.shape[1] // 2
+
+    def along_y(ty, tz, slot):
+        return remote(
+            out_y.at[ty, tz],
+            in_y.at[slot, tz],
+            box_send.at[ty * 4 + tz],
+            box_recv.at[slot * 4 + tz],
+            "sec",
+            mz * 4 + ty,
+        )
+
+    def along_z(tz, ty, slot):
+        return remote(
+            out_z.at[tz, ty],
+            in_z.at[slot, ty],
+            box_send.at[16 + tz * 4 + ty],
+            box_recv.at[16 + slot * 4 + ty],
+            "sec",
+            tz * 4 + my,
+        )
+
+    def on_z(tz, slot):
+        return remote(
+            mid_out.at[0, tz],
+            mid_in.at[0, slot],
+            mid_send.at[tz],
+            mid_recv.at[slot],
+            "sec",
+            tz * 4 + my,
+        )
+
+    def on_y(ty, slot):
+        return remote(
+            mid_out.at[1, ty],
+            mid_in.at[1, slot],
+            mid_send.at[4 + ty],
+            mid_recv.at[4 + slot],
+            "sec",
+            mz * 4 + ty,
+        )
+
     def pool(i, _):
-        first = 2 * lax.rem(me // 2 + 1 + i, n // 2)
-        hot = jnp.where(
-            lax.broadcasted_iota(jnp.int32, (2 * TOKB, cells), 0) == (gid_ref[...] - first * TOKB),
-            1.0,
-            0.0,
-        ).astype(BF16)
+        peers = [
+            moved(me, *(pick(i, [step[one][axis] for step in ORDER]) for axis in range(2)))
+            for one in range(2)
+        ]
+        hot = jnp.concatenate(
+            [
+                jnp.where(
+                    lax.broadcasted_iota(jnp.int32, (TOKB, cells), 0)
+                    == (gid_ref[...] - peer * TOKB),
+                    1.0,
+                    0.0,
+                ).astype(BF16)
+                for peer in peers
+            ],
+            axis=0,
+        )
         both = dot(hot, enc[...]).astype(BF16)
         for one in range(2):
-            peer = first + one
+            tz, ty = peers[one] // 4, lax.rem(peers[one], 4)
             part = both[one * TOKB : (one + 1) * TOKB]
-
-            @pl.when(peer != me)
+            near, far = part[:, :wide], part[:, wide:]
+
+            @pl.when(ty != my)
             def _():
-                outbox[peer] = part
-                remote(
-                    outbox.at[peer], inbox.at[me], box_send.at[peer], box_recv.at[me], "sec", peer
-                ).start()
-                remote(
-                    cnt_out.at[peer], cnt_in.at[me], cnt_send.at[peer], cnt_recv.at[me], "sec", peer
-                ).start()
-
-            @pl.when(peer == me)
+                out_y[ty, tz] = near
+                along_y(ty, tz, my).start()
+
+            @pl.when(ty == my)
             def _():
-                inbox[me] = part
-                cnt_in[me] = cnt_out[me]
+                in_y[my, tz] = near
+
+            @pl.when(tz != mz)
+            def _():
+                out_z[tz, ty] = far
+                along_z(tz, ty, mz).start()
+
+            @pl.when(tz == mz)
+            def _():
+                in_z[mz, ty] = far
 
         return 0
 
     lax.fori_loop(0, n // 2, pool, 0)
+
+    row = gid_ref[...]
+    tok_hot = jnp.where(
+        lax.broadcasted_iota(jnp.int32, (TOKB, cells), 0) == (row & (TOKB - 1)), 1.0, 0.0
+    ).astype(BF16)
+    cyc_hot = jnp.where(
+        lax.broadcasted_iota(jnp.int32, (n, cells), 0) == (row >> 8), 1.0, 0.0
+    ).astype(BF16)
+    hist = dot_nt(cyc_hot, tok_hot)
+    for r in range(n):
+        cnt_out[r] = hist[r : r + 1, :]
+
+    def send_counts(peer):
+        remote(
+            cnt_out.at[peer], cnt_in.at[me], cnt_send.at[peer], cnt_recv.at[me], "sec", peer
+        ).start()
+
+    each_peer(n, me, send_counts)
+    cnt_in[me] = cnt_out[me]
 
     last = values.shape[1] - HEAD
     ones = jnp.where(
@@ -266,23 +370,60 @@
         values[c, HEAD:, :] = ones
     accs[...] = jnp.zeros_like(accs)
 
+    def first_hop(j, _):
+        ty, tz = lax.rem(my + j, 4), lax.rem(mz + j, 4)
+        for other in range(4):
+            along_y(ty, other, ty).wait()
+            along_z(tz, other, tz).wait()
+        return 0
+
+    lax.fori_loop(1, 4, first_hop, 0)
+
+    def added(ref, k):
+        total = ref[0, k].astype(F32)
+        for r in range(1, 4):
+            total = total + ref[r, k].astype(F32)
+        return total
+
+    def second_hop(j, _):
+        ty, tz = lax.rem(my + j, 4), lax.rem(mz + j, 4)
+        mid_out[0, tz] = added(in_y, tz)
+        on_z(tz, mz).start()
+        mid_out[1, ty] = added(in_z, ty)
+        on_y(ty, my).start()
+        return 0
+
+    lax.fori_loop(1, 4, second_hop, 0)
+    mid_in[0, mz] = added(in_y, mz)
+    mid_in[1, my] = added(in_z, my)
+
     def arrive(peer):
         remote(
             cnt_out.at[peer], cnt_in.at[peer], cnt_send.at[peer], cnt_recv.at[peer], "sec", peer
         ).wait()
-        remote(
-            outbox.at[peer], inbox.at[peer], box_send.at[peer], box_recv.at[peer], "sec", peer
-        ).wait()
 
     each_peer(n, me, arrive)
+
+    def last_hop(j, _):
+        ty, tz = lax.rem(my + j, 4), lax.rem(mz + j, 4)
+        on_z(tz, tz).wait()
+        on_y(ty, ty).wait()
+        return 0
+
+    lax.fori_loop(1, 4, last_hop, 0)
+    counts = cnt_in[0]
+    for r in range(1, n):
+        counts = counts + cnt_in[r]
+    halves = []
+    for h in range(2):
+        total = mid_in[h, 0]
+        for r in range(1, 4):
+            total = total + mid_in[h, r]
+        halves.append(total)
+    sums = jnp.concatenate(halves, axis=1)
     loads[2].wait()
     loads[3].wait()
-    sums = inbox[0].astype(F32)
-    counts = cnt_in[0]
-    for r in range(1, n):
-        sums = sums + inbox[r].astype(F32)
-        counts = counts + cnt_in[r]
-    root = jnp.sqrt(jnp.transpose(counts)[:, 0:1] + 1.0)
+    root = jnp.sqrt(jnp.transpose(jnp.broadcast_to(counts, (8, TOKB)))[:, 0:1] + 1.0)
     pooled = (sums / root).astype(BF16)
     lifted = dot(pooled, in_w[...])
     normed_ref[...] = (
@@ -293,75 +434,97 @@
     half = TOKB // 2
     planes = HEADS // 4
 
-    def project(i, _):
-        group = lax.rem(me // 4 + i, planes)
-        column = group * (4 * HEAD)
-        q4, k4, v4 = (
-            dot(
-                normed_ref[...],
-                qkv_w[:, pl.ds(pl.multiple_of(part * D + column, 4 * HEAD), 4 * HEAD)],
-            )
-            for part in range(3)
+    def place(group, one, sign):
+        dz, dy = (pick(group, [g[one][axis] for g in GROUPS]) for axis in range(2))
+        return moved(me, sign * dz, sign * dy)
+
+    def message(peer, slot):
+        return remote(
+            outmsg.at[peer], inmsg.at[slot], msg_send.at[peer], msg_recv.at[slot], "sec", peer
         )
-        q4 = q4 * HEAD ** (-0.5)
-        vt = jnp.transpose(v4).astype(BF16)
+
+    def send_group(group):
         for one in range(4):
-            peer = group * 4 + one
-            lanes = slice(one // 2 * 128, one // 2 * 128 + 128)
-            q, k = q4[:, lanes], k4[:, lanes]
-            if one % 2 == 0:
-                packed = jnp.where(low, q, swap_halves(k))
-            else:
-                packed = jnp.where(low, swap_halves(q), k)
-            outmsg[peer, 0:TOKB] = packed.astype(BF16)
-            mine = vt[one * HEAD : (one + 1) * HEAD]
-            outmsg[peer, TOKB : TOKB + HEAD] = mine[:, :half]
-            outmsg[peer, TOKB + HEAD : TOKB + 2 * HEAD] = mine[:, half:]
+            peer = place(group, one, 1)
 
             @pl.when(peer != me)
             def _():
-                remote(
-                    outmsg.at[peer], inmsg.at[me], msg_send.at[peer], msg_recv.at[me], "sec", peer
-                ).start()
+                message(peer, me).start()
 
             @pl.when(peer == me)
             def _():
                 inmsg[me] = outmsg[me]
 
-        return 0
-
-    lax.fori_loop(0, planes, project, 0)
+    def sent_group(group):
+        for one in range(4):
+            peer = place(group, one, 1)
+
+            @pl.when(peer != me)
+            def _():
+                message(peer, me).wait_send()
+
+    def project(i, _):
+        for j in range(2):
+            group = lax.rem(me // 4 + planes + pick(i, [two[j] for two in PLANES]), planes)
+            column = group * (4 * HEAD)
+            q4, k4, v4 = (
+                dot(
+                    normed_ref[...],
+                    qkv_w[:, pl.ds(pl.multiple_of(part * D + column, 4 * HEAD), 4 * HEAD)],
+                )
+                for part in range(3)
+            )
+            q4 = q4 * HEAD ** (-0.5)
+            vt = jnp.transpose(v4).astype(BF16)
+            for one in range(4):
+                head = group * 4 + one
+                lanes = slice(one // 2 * 128, one // 2 * 128 + 128)
+                q, k = q4[:, lanes], k4[:, lanes]
+                if one % 2 == 0:
+                    packed = jnp.where(low, q, swap_halves(k))
+                else:
+                    packed = jnp.where(low, swap_halves(q), k)
+                outmsg[head, 0:TOKB] = packed.astype(BF16)
+                mine = vt[one * HEAD : (one + 1) * HEAD]
+                outmsg[head, TOKB : TOKB + HEAD] = mine[:, :half]
+                outmsg[head, TOKB + HEAD : TOKB + 2 * HEAD] = mine[:, half:]
+
+        @pl.when(i == 0)
+        def _():
+            send_group(0)
+
+        return 0
+
+    lax.fori_loop(0, len(PLANES), project, 0)
+    for group in range(1, WINDOW):
+        send_group(group)
 
     def meet(q, k):
         acc = accs[q]
         for c in range(2):
-            first = k * 4 + 2 * c
-            key = jnp.concatenate([inmsg[first, 0:TOKB], inmsg[first + 1, 0:TOKB]], axis=0)
+            key = keys[k, c * 2 * TOKB : (c + 1) * 2 * TOKB]
             expo = jnp.exp2(dot_nt(key, queries[q]) * LOG2E).astype(BF16)
             acc = acc + dot(values[k * 2 + c], expo)
         accs[q] = acc
 
     def stage(i, _):
-        plane = lax.rem(me // 4 + planes - i, planes)
+        @pl.when(i + WINDOW < planes)
+        def _():
+            sent_group(i)
+            send_group(i + WINDOW)
+
         for one in range(4):
-            peer = plane * 4 + one
+            peer = place(i, one, -1)
 
             @pl.when(peer != me)
             def _():
-                remote(
-                    outmsg.at[peer],
-                    inmsg.at[peer],
-                    msg_send.at[peer],
-                    msg_recv.at[peer],
-                    "sec",
-                    peer,
-                ).wait_recv()
-
-            qk = inmsg[peer, 0:TOKB].astype(F32)
-            queries[plane, one * TOKB : (one + 1) * TOKB] = jnp.where(
-                low, 0.0, swap_halves(qk)
-            ).astype(BF16)
-            chunk = plane * 2 + one // 2
+                message(peer, peer).wait_recv()
+
+            span = slice(one * TOKB, (one + 1) * TOKB)
+            qk = inmsg[peer, 0:TOKB]
+            keys[i, span] = qk
+            queries[i, span] = jnp.where(low, 0.0, swap_halves(qk.astype(F32))).astype(BF16)
+            chunk = i * 2 + one // 2
             base = one % 2 * TOKB
             values[chunk, 0:HEAD, base : base + half] = inmsg[peer, TOKB : TOKB + HEAD]
             values[chunk, 0:HEAD, base + half : base + TOKB] = inmsg[
@@ -370,17 +533,15 @@
 
         def pair(t, _):
             fresh = t >= i
-            back_q = jnp.where(fresh, i, t)
-            back_k = jnp.where(fresh, t - i, i)
-            q = lax.rem(me // 4 + planes - back_q, planes)
-            meet(q, lax.rem(me // 4 + planes - back_k, planes))
+            q = jnp.where(fresh, i, t)
+            meet(q, jnp.where(fresh, t - i, i))
 
             @pl.when((i == planes - 1) & ((t < i) | (t == 2 * i)))
             def _():
                 acc = accs[q]
                 ctx = (acc[:HEAD] / acc[HEAD : HEAD + 1]).astype(BF16)
                 for one in range(4):
-                    peer = q * 4 + one
+                    peer = place(q, one, -1)
                     mine = ctx[:, one * TOKB : (one + 1) * TOKB]
 
                     @pl.when(peer != me)
@@ -406,10 +567,10 @@
 
     lax.fori_loop(0, planes, stage, 0)
 
+    for group in range(planes - WINDOW, planes):
+        sent_group(group)
+
     def context(peer):
-        remote(
-            outmsg.at[peer], inmsg.at[peer], msg_send.at[peer], msg_recv.at[peer], "sec", peer
-        ).wait_send()
         remote(
             outctx.at[peer], inctx.at[peer], ctx_send.at[peer], ctx_recv.at[peer], "sec", peer
         ).wait()
@@ -600,13 +761,18 @@
             pltpu.VMEM((1, cells), jnp.int32),
             pltpu.VMEM((cells + 2 * beams, width), BF16),
             pltpu.VMEM((cells, width), BF16),
-            pltpu.VMEM((n, TOKB, width), BF16),
-            pltpu.VMEM((n, TOKB, width), BF16),
-            pltpu.VMEM((n, 8, TOKB), F32),
-            pltpu.VMEM((n, 8, TOKB), F32),
+            pltpu.VMEM((4, 4, TOKB, width // 2), BF16),
+            pltpu.VMEM((4, 4, TOKB, width // 2), BF16),
+            pltpu.VMEM((4, 4, TOKB, width // 2), BF16),
+            pltpu.VMEM((4, 4, TOKB, width // 2), BF16),
+            pltpu.VMEM((2, 4, TOKB, width // 2), F32),
+            pltpu.VMEM((2, 4, TOKB, width // 2), F32),
+            pltpu.VMEM((n, 1, TOKB), F32),
+            pltpu.VMEM((n, 1, TOKB), F32),
             pltpu.VMEM(message, BF16),
             pltpu.VMEM(message, BF16),
             pltpu.VMEM((TOKB, D), BF16),
+            pltpu.VMEM((n // 4, 4 * TOKB, 128), BF16),
             pltpu.VMEM((n // 4, 4 * TOKB, 128), BF16),
             pltpu.VMEM((n // 2, HEAD + 16, 2 * TOKB), BF16),
             pltpu.VMEM((n // 4, HEAD + 16, 4 * TOKB), F32),
@@ -630,8 +796,10 @@
             dma(7),
             dma(2),
             dma(2),
-            dma(n),
-            dma(n),
+            dma(32),
+            dma(32),
+            dma(8),
+            dma(8),
             dma(n),
             dma(n),
             dma(n),

time: 114 us -> 103 us (0.904)
  Pallas kernels: 113 us -> 102 us
    pallas_call x1, Pallas kernels: 112 us -> 100 us  [shards(): pl.pallas_call(functools.partial(forecast_kernel, n, nd, cells, beams), o...]
where the time goes in v3:
time: 103 us; the launch traced here: 102 us
  Pallas kernels  102 us (99%)
    pallas_call x1, Pallas kernels, shards(): pl.pallas_call(functools.partial(forecast_kernel, n, nd, cells, beams), o...  100 us

profile of v3, /device:TPU:1, one launch (start us, length us, event | category | flops | bytes accessed | tf_op | source)
XLA Modules:
  0.0 102.5 jit_solution(10876940037230185497)
XLA Ops:
  0.6 100.3 %forecast.1 = (f32[16,8,128]{2,1,0:T(8,128)}, f32[16,8,128]{2,1,0:T(8,128)}) custom-call(s32[4,128]{1,0:T(4,128)} %bitcast.14, s32[64,64]{1,0:T(8,128)} %bitcast.11, s32[64,64]{1,0:T(8,128)} %tok_ref.1, bf16[16,1024]{1,0:T(8,128)(2,1)} %bitcast.12, bf16[16,256]{1,0:T(8,128)(2,1)} %bitcast.13, bf16[4096,256]{1,0:T(8,128)(2,1)} %bitcast.10, ...), custom_call_target="tpu_custom_call" | custom-call | tf_op jit(solution)/shard_map/forecast/pallas_call | solution.py:752
  101.0 1.5 %finish.1 = (f32[8,128]{1,0:T(8,128)}, f32[16,1024]{1,0:T(8,128)}) custom-call(f32[16,8,128]{2,1,0:T(8,128)} %get-tuple-element.6.tau_ref, f32[16,8,128]{2,1,0:T(8,128)} %get-tuple-element.7.full_ref), custom_call_target="tpu_custom_call" | custom-call | tf_op jit(solution)/shard_map/finish/pallas_call | solution.py:836

commit v4 on v3

--- a/solution.py
+++ b/solution.py
@@ -619,29 +619,32 @@
     factor = 4.0 / (n * KB * 128)
 
     def render(i, _):
-        peer = lax.rem(me + i, n)
-        for y in range(owned):
-            bundle = peer * owned + y
-            ray = rays[pl.ds(pl.multiple_of(bundle * 128, 128), 128), :]
-            picks = [ids[j, bundle] for j in range(KB)]
-            score = dot_nt(jnp.concatenate([vox[b] for b in picks], axis=0), ray)
-            total = jnp.zeros((8, 128), F32)
-            for j in range(KB):
-                value = softplus(score[j * 128 : (j + 1) * 128]) * dens[picks[j]]
-                total = total + jnp.sum(value.reshape(16, 8, 128), axis=0)
-            tau_out[peer, y : y + 1, :] = jnp.sum(total, axis=0, keepdims=True) * factor
-
-        @pl.when(i < n)
-        def _():
-            remote(
-                tau_out.at[peer], tau_in.at[me], tau_send.at[peer], tau_recv.at[me], "sec", peer
-            ).start()
-
-        @pl.when(i == n)
-        def _():
-            tau_in[me] = tau_out[me]
-
-        @pl.when(i == 3)
+        peers = [lax.rem(me + 2 * i + 1 + one, n) for one in range(2)]
+        for peer in peers:
+            for y in range(owned):
+                bundle = peer * owned + y
+                ray = rays[pl.ds(pl.multiple_of(bundle * 128, 128), 128), :]
+                picks = [ids[j, bundle] for j in range(KB)]
+                score = dot_nt(jnp.concatenate([vox[b] for b in picks], axis=0), ray)
+                total = jnp.zeros((8, 128), F32)
+                for j in range(KB):
+                    value = softplus(score[j * 128 : (j + 1) * 128]) * dens[picks[j]]
+                    total = total + jnp.sum(value.reshape(16, 8, 128), axis=0)
+                tau_out[peer, y : y + 1, :] = jnp.sum(total, axis=0, keepdims=True) * factor
+
+        for peer in peers:
+
+            @pl.when(peer != me)
+            def _():
+                remote(
+                    tau_out.at[peer], tau_in.at[me], tau_send.at[peer], tau_recv.at[me], "sec", peer
+                ).start()
+
+            @pl.when(peer == me)
+            def _():
+                tau_in[me] = tau_out[me]
+
+        @pl.when(i == 1)
         def _():
             def wait_part(peer):
                 remote(
@@ -667,7 +670,7 @@
 
             each_peer(nd, clip, send_row)
 
-        @pl.when(i == 8)
+        @pl.when(i == 4)
         def _():
             def wait_row(peer):
                 remote(
@@ -690,7 +693,7 @@
 
         return 0
 
-    lax.fori_loop(1, n + 1, render, 0)
+    lax.fori_loop(0, n // 2, render, 0)
 
     def finish(peer):
         remote(

time: 103 us -> 102 us (level)
  Pallas kernels: 102 us -> 100 us
    pallas_call x1, Pallas kernels: 100 us -> 98.6 us  [shards(): pl.pallas_call(functools.partial(forecast_kernel, n, nd, cells, beams), o...]
where the time goes in v4:
time: 102 us; the launch traced here: 101 us
  Pallas kernels  100 us (98%)
    pallas_call x1, Pallas kernels, shards(): pl.pallas_call(functools.partial(forecast_kernel, n, nd, cells, beams), o...  98.6 us

profile of v4, /device:TPU:1, one launch (start us, length us, event | category | flops | bytes accessed | tf_op | source)
XLA Modules:
  0.0 100.8 jit_solution(7534163746952529726)
XLA Ops:
  0.6 98.6 %forecast.1 = (f32[16,8,128]{2,1,0:T(8,128)}, f32[16,8,128]{2,1,0:T(8,128)}) custom-call(s32[4,128]{1,0:T(4,128)} %bitcast.14, s32[64,64]{1,0:T(8,128)} %bitcast.11, s32[64,64]{1,0:T(8,128)} %tok_ref.1, bf16[16,1024]{1,0:T(8,128)(2,1)} %bitcast.12, bf16[16,256]{1,0:T(8,128)(2,1)} %bitcast.13, bf16[4096,256]{1,0:T(8,128)(2,1)} %bitcast.10, ...), custom_call_target="tpu_custom_call" | custom-call | tf_op jit(solution)/shard_map/forecast/pallas_call | solution.py:755
  99.3 1.5 %finish.1 = (f32[8,128]{1,0:T(8,128)}, f32[16,1024]{1,0:T(8,128)}) custom-call(f32[16,8,128]{2,1,0:T(8,128)} %get-tuple-element.6.tau_ref, f32[16,8,128]{2,1,0:T(8,128)} %get-tuple-element.7.full_ref), custom_call_target="tpu_custom_call" | custom-call | tf_op jit(solution)/shard_map/finish/pallas_call | solution.py:839

commit v5 on v4

--- a/solution.py
+++ b/solution.py
@@ -499,13 +499,12 @@
     for group in range(1, WINDOW):
         send_group(group)
 
-    def meet(q, k):
-        acc = accs[q]
+    def meet(acc, q, k):
         for c in range(2):
             key = keys[k, c * 2 * TOKB : (c + 1) * 2 * TOKB]
             expo = jnp.exp2(dot_nt(key, queries[q]) * LOG2E).astype(BF16)
             acc = acc + dot(values[k * 2 + c], expo)
-        accs[q] = acc
+        return acc
 
     def stage(i, _):
         @pl.when(i + WINDOW < planes)
@@ -532,11 +531,20 @@
             ]
 
         def pair(t, _):
-            fresh = t >= i
-            q = jnp.where(fresh, i, t)
-            meet(q, jnp.where(fresh, t - i, i))
-
-            @pl.when((i == planes - 1) & ((t < i) | (t == 2 * i)))
+            q = t
+
+            @pl.when(t < i)
+            def _():
+                older, newer = accs[t], accs[i]
+                older, newer = meet(older, t, i), meet(newer, i, t)
+                accs[t] = older
+                accs[i] = newer
+
+            @pl.when(t == i)
+            def _():
+                accs[i] = meet(accs[i], i, i)
+
+            @pl.when(i == planes - 1)
             def _():
                 acc = accs[q]
                 ctx = (acc[:HEAD] / acc[HEAD : HEAD + 1]).astype(BF16)
@@ -562,7 +570,7 @@
 
             return 0
 
-        lax.fori_loop(0, 2 * i + 1, pair, 0)
+        lax.fori_loop(0, i + 1, pair, 0)
         return 0
 
     lax.fori_loop(0, planes, stage, 0)

time: 102 us -> 101 us (level)
  no operation moved by 1% of the time
where the time goes in v5:
time: 101 us; the launch traced here: 100 us
  Pallas kernels  99.6 us (99%)
    pallas_call x1, Pallas kernels, shards(): pl.pallas_call(functools.partial(forecast_kernel, n, nd, cells, beams), o...  98.1 us

profile of v5, /device:TPU:1, one launch (start us, length us, event | category | flops | bytes accessed | tf_op | source)
XLA Modules:
  0.0 100.3 jit_solution(5592328797779528336)
XLA Ops:
  0.6 98.1 %forecast.1 = (f32[16,8,128]{2,1,0:T(8,128)}, f32[16,8,128]{2,1,0:T(8,128)}) custom-call(s32[4,128]{1,0:T(4,128)} %bitcast.14, s32[64,64]{1,0:T(8,128)} %bitcast.11, s32[64,64]{1,0:T(8,128)} %tok_ref.1, bf16[16,1024]{1,0:T(8,128)(2,1)} %bitcast.12, bf16[16,256]{1,0:T(8,128)(2,1)} %bitcast.13, bf16[4096,256]{1,0:T(8,128)(2,1)} %bitcast.10, ...), custom_call_target="tpu_custom_call" | custom-call | tf_op jit(solution)/shard_map/forecast/pallas_call | solution.py:763
  98.8 1.5 %finish.1 = (f32[8,128]{1,0:T(8,128)}, f32[16,1024]{1,0:T(8,128)}) custom-call(f32[16,8,128]{2,1,0:T(8,128)} %get-tuple-element.6.tau_ref, f32[16,8,128]{2,1,0:T(8,128)} %get-tuple-element.7.full_ref), custom_call_target="tpu_custom_call" | custom-call | tf_op jit(solution)/shard_map/finish/pallas_call | solution.py:847
